TPU v7x, 512 devices: a whole 4x4x16 slice. The times are simulated.
512 devices in a mesh: tm: 32 (over y, z_lo, core), rows: 16 (over z_hi, x).
Axes of the slice: x: 4, y: 4, z: 16 (z_hi: 4, z_lo: 4; z = z_hi * 4 + z_lo), core: 2. Of those that a mesh axis runs over, the one named last changes fastest.
Arguments:
- latent_features: bfloat16 [64, 16, 160, 384], P('tm', 'rows'), may hold values from -6 to 6
- attn_gain: float32 [384], replicated, may hold values from 0.1 to 1.9
- w_query: bfloat16 [384, 384], replicated
- w_key: bfloat16 [384, 384], replicated, may hold values from -0.3125 to 0.3125
- w_value: bfloat16 [384, 384], replicated, may hold values from -0.3125 to 0.3125
- w_proj: bfloat16 [384, 384], replicated, may hold values from -0.3125 to 0.3125
- unit_gain: float32 [384], replicated, may hold values from 0.1 to 1.9
- conv_weight: bfloat16 [3, 3, 3, 384, 384], P(None, None, None, 'rows'), may hold values from -0.0625 to 0.0625
- upsample_weight: bfloat16 [3, 384, 768], replicated, may hold values from -0.1875 to 0.1875
Outputs:
- upsampled: bfloat16 [128, 16, 160, 384], P('tm', 'rows')
All inputs are finite; a program needn't handle non-finite values.
Results may differ from a plain program's by a relative error of at most 0.015.
The roundings to bfloat16 on the way count: a program that leaves them out, or rounds other values in their place, can miss the bound.
Values may be sent and summed in bfloat16 or wider, within the bound.
A program may use at most 64 MiB of HBM per device.

v0:
```python
import math

import jax
import jax.numpy as jnp
from jax import lax
from jax.sharding import PartitionSpec as P

epsilon = 1e-06


def extended_2(cells, sides, width):
    for axis, dim in sides:
        count = lax.axis_size(axis)
        ends = count - 1
        head = lax.slice_in_dim(cells, 0, width, axis=dim)
        tail = lax.slice_in_dim(cells, cells.shape[dim] - width, cells.shape[dim], axis=dim)
        cells = jnp.concatenate(
            [
                lax.ppermute(tail, axis, [(i, (i + 1) % count) for i in range(ends)]),
                cells,
                lax.ppermute(head, axis, [((i + 1) % count, i) for i in range(ends)]),
            ],
            axis=dim,
        )
    return cells


def shifted(value, axis, steps):
    count = lax.axis_size(axis)
    leading, last = (max(0, -steps), min(count, count - steps))
    return lax.ppermute(value, axis, [(source, source + steps) for source in range(leading, last)])


def rms_scale(values, gain):
    widened = values.astype(jnp.float32)
    return widened * lax.rsqrt(jnp.mean(widened * widened, axis=-1, keepdims=True) + epsilon) * gain


def volume_conv(extended, kernel):
    return lax.conv_general_dilated(
        extended[None],
        kernel,
        (1, 1, 1),
        ((0, 0), (0, 0), (1, 1)),
        dimension_numbers=("NDHWC", "DHWIO", "NDHWC"),
        preferred_element_type=jnp.float32,
    )[0]


def time_conv(extended, kernel):
    frames = extended.shape[0] - 2
    stretched = jnp.dot(extended[0:frames], kernel[0], preferred_element_type=jnp.float32)
    stretched = stretched + jnp.dot(
        extended[1 : frames + 1], kernel[1], preferred_element_type=jnp.float32
    )
    stretched = stretched + jnp.dot(
        extended[2 : frames + 2], kernel[2], preferred_element_type=jnp.float32
    )
    return stretched


def alternate(stretched):
    frames, rows_here, columns, doubled = stretched.shape
    channels = doubled // 2
    split_up = stretched.reshape(frames, rows_here, columns, 2, channels)
    split_up = jnp.transpose(split_up, (0, 3, 1, 2, 4))
    return split_up.reshape(2 * frames, rows_here, columns, channels).astype(jnp.bfloat16)


def rim_conv(extended, conv_weight):
    rimmed = extended_2(extended, (("rows", 1),), 1)
    out_frames = extended.shape[0] - 2
    initial = jnp.zeros(
        (out_frames, extended.shape[1], extended.shape[2], conv_weight.shape[4]), jnp.float32
    )
    return initial + volume_conv(rimmed, lax.all_gather(conv_weight, "rows", axis=3, tiled=True))


def body(
    latent_features,
    attn_gain,
    w_query,
    w_key,
    w_value,
    w_proj,
    unit_gain,
    conv_weight,
    upsample_weight,
):
    frames, rows_here, columns, channels = latent_features.shape
    score_scale = 1.0 / math.sqrt(channels)
    normed = rms_scale(latent_features, attn_gain).astype(jnp.bfloat16)
    flattened = normed.reshape(frames, rows_here * columns, channels)
    queries = jnp.dot(flattened, w_query, preferred_element_type=jnp.float32).astype(jnp.bfloat16)
    key_local = jnp.dot(flattened, w_key, preferred_element_type=jnp.float32).astype(jnp.bfloat16)
    value_local = jnp.dot(flattened, w_value, preferred_element_type=jnp.float32).astype(
        jnp.bfloat16
    )
    key_local = key_local.reshape(frames, rows_here, columns, channels)
    value_local = value_local.reshape(frames, rows_here, columns, channels)
    key_block = lax.all_gather(key_local, "rows", axis=1, tiled=True).reshape(frames, -1, channels)
    value_block = lax.all_gather(value_local, "rows", axis=1, tiled=True).reshape(
        frames, -1, channels
    )
    running_max = jnp.full((frames, rows_here * columns), -jnp.inf, jnp.float32)
    weight_sum = jnp.zeros((frames, rows_here * columns), jnp.float32)
    numerator = jnp.zeros((frames, rows_here * columns, channels), jnp.float32)
    scores = (
        jnp.einsum("fqc,fkc->fqk", queries, key_block, preferred_element_type=jnp.float32)
        * score_scale
    )
    new_max = jnp.max(scores, axis=-1)
    rescale = jnp.exp(running_max - new_max)
    weights = jnp.exp(scores - new_max[..., None])
    weight_sum = weight_sum * rescale + jnp.sum(weights, axis=-1)
    numerator = numerator * rescale[..., None] + jnp.einsum(
        "fqk,fkc->fqc", weights, value_block.astype(jnp.float32), precision=lax.Precision.HIGHEST
    )
    attn_mixed = (numerator / weight_sum[..., None]).astype(jnp.bfloat16)
    projected = jnp.dot(attn_mixed, w_proj, preferred_element_type=jnp.float32)
    attended = (
        latent_features.astype(jnp.float32)
        + projected.reshape(frames, rows_here, columns, channels)
    ).astype(jnp.bfloat16)
    activated = jax.nn.silu(rms_scale(attended, unit_gain)).astype(jnp.bfloat16)
    earlier = shifted(activated, "tm", 1)
    conv_out = rim_conv(jnp.concatenate([earlier, activated], axis=0), conv_weight)
    unit_out = (attended.astype(jnp.float32) + conv_out).astype(jnp.bfloat16)
    earlier_out = shifted(unit_out[frames - 2 :], "tm", 1)
    unit_extended = jnp.concatenate([earlier_out, unit_out], axis=0)
    return alternate(time_conv(unit_extended, upsample_weight))


def solution(mesh):
    in_specs = (
        P("tm", "rows", None, None),
        P(),
        P(),
        P(),
        P(),
        P(),
        P(),
        P(None, None, None, "rows", None),
        P(),
    )
    out_specs = P("tm", "rows", None, None)
    return jax.shard_map(body, mesh=mesh, in_specs=in_specs, out_specs=out_specs, check_vma=False)
```

profile of v0, /device:TPU:24, one launch (start us, length us, event | category | flops | bytes accessed | tf_op | source)
XLA Modules:
  0.0 542.7 jit_solution(3032713576060827479)
XLA Ops:
  6.5 1.1 fusion.32
  7.7 2.2 convolution_convert_fusion.1
  10.0 2.2 convolution_convert_fusion
  12.2 0.7 all-gather.6.cloned.1.call-update
  12.9 131.0 %all-gather.8.cloned.1.call-done = bf16[2,2560,384]{2,1,0:T(8,128)(2,1)} async-done(((bf16[2,160,384]{2,1,0:T(8,128)(2,1)}), bf16[2,2560,384]{2,1,0:T(8,128)(2,1)}) %all-gather.8.cloned.1.call-update) | async-done | bytes 3932176 | tf_op jit(solution)/shard_map/all_gather | solution.py:101
  143.9 5.6 %fusion.58 = (f32[2,160]{1,0:T(2,128)S(1)}, f32[2,160,2560]{2,1,0:T(8,128)}) fusion(bf16[2,2560,384]{2,1,0:T(8,128)(2,1)} %all-gather.8.cloned.1.call-done, bf16[384,384]{1,0:T(8,128)(2,1)S(1)} %copy-done, bf16[2,1,160,384]{3,2,1,0:T(8,128)(2,1)} %param.9, f32[384]{0:T(512)} %param.10, f32[2,160]{1,0:T(2,128)S(1)} %add_rsqrt_fusion.1), kind=kOutput, calls=%fused_computation.69 | convolution fusion | flops 725769920 | bytes 7753728 | tf_op jit(solution)/shard_map/fqc,fkc->fqk/dot_general | solution.py:109
  149.5 2.5 fusion.1
  152.0 118.9 %all-gather.10.cloned.1.call-done = bf16[2,2560,384]{2,1,0:T(8,128)(2,1)} async-done(((bf16[2,160,384]{2,1,0:T(8,128)(2,1)}), bf16[2,2560,384]{2,1,0:T(8,128)(2,1)}) %all-gather.10.cloned.1.call-update) | async-done | bytes 3932176 | tf_op jit(solution)/shard_map/all_gather | solution.py:102
  271.0 6.0 %fusion.22 = bf16[2,160,384]{2,1,0:T(8,128)(2,1)S(1)} fusion(bf16[2,2560,384]{2,1,0:T(8,128)(2,1)} %all-gather.10.cloned.1.call-done, f32[2,160,2560]{2,1,0:T(8,128)} %get-tuple-element.10, f32[2,160]{1,0:T(2,128)S(1)} %get-tuple-element.9, f32[2,160]{1,0:T(2,128)S(1)} %get-tuple-element.8, f32[2,160]{1,0:T(2,128)S(1)} %get-tuple-element.7), kind=kOutput, calls=%fused_computation.28 | convolution fusion | flops 3776061440 | bytes 7458560 | tf_op jit(solution)/shard_map/fqk,fkc->fqc/dot_general | solution.py:116
  277.0 0.4 multiply_reduce_fusion
  277.6 1.9 collective-permute-start
  279.6 8.3 %collective-permute-done = bf16[2,1,160,384]{3,2,0,1:T(8,128)(2,1)S(1)} collective-permute-done((bf16[2,1,160,384]{3,2,0,1:T(8,128)(2,1)S(1)}, bf16[2,1,160,384]{3,2,0,1:T(8,128)(2,1)S(1)}, u32[]{:S(2)}, u32[]{:S(2)}) %collective-permute-start) | collective-permute-done | bytes 245792 | tf_op jit(solution)/shard_map/ppermute | solution.py:31
  287.9 4.4 collective-permute-start.1
  292.3 1.5 collective-permute-start.2
  293.8 7.5 %collective-permute-done.1 = bf16[4,1,160,384]{3,2,0,1:T(8,128)(2,1)S(1)} collective-permute-done((bf16[4,1,160,384]{3,2,0,1:T(8,128)(2,1)S(1)}, bf16[4,1,160,384]{3,2,0,1:T(8,128)(2,1)S(1)}, u32[]{:S(2)}, u32[]{:S(2)}) %collective-permute-start.1) | collective-permute-done | bytes 491552 | tf_op jit(solution)/shard_map/ppermute | solution.py:19
  301.2 3.1 collective-permute-done.2
  304.5 0.8 copy.23
  305.3 0.6 pad.clone
  306.1 210.5 %all-gather.6.cloned.1.call-done = bf16[3,3,3,384,384]{4,3,2,1,0:T(8,128)(2,1)} async-done(((bf16[3,3,3,24,384]{4,3,2,1,0:T(8,128)(2,1)}), bf16[3,3,3,384,384]{4,3,2,1,0:T(8,128)(2,1)}) %all-gather.6.cloned.1.call-update) | async-done | bytes 7962640 | tf_op jit(solution)/shard_map/all_gather | solution.py:76
  516.6 7.1 %fusion.14 = f32[2,1,8,21,384]{4,2,3,1,0:T(8,128)S(1)} fusion(bf16[3,3,3,384,384]{4,3,2,1,0:T(8,128)(2,1)} %all-gather.6.cloned.1.call-done, bf16[4,3,1,7,2,384]{5,3,4,1,0,2:T(8,128)(2,1)S(1)} %slice.28, bf16[4,3,1,8,21,384]{5,3,4,1,0,2:T(8,128)(2,1)S(1)} %copy.17, pred[8,21]{0,1:T(8,128)(4,1)S(1)} %copy-done.5), kind=kOutput, calls=%fused_computation.19 | convolution fusion | flops 2680657920 | bytes 10156200 | tf_op jit(solution)/shard_map/conv_general_dilated | solution.py:40
  524.2 1.9 collective-permute-start.3
  526.5 7.9 %collective-permute-done.3 = bf16[2,1,160,384]{3,2,0,1:T(8,128)(2,1)S(1)} collective-permute-done((bf16[2,1,160,384]{3,2,0,1:T(8,128)(2,1)S(1)}, bf16[2,1,160,384]{3,2,0,1:T(8,128)(2,1)S(1)}, u32[]{:S(2)}, u32[]{:S(2)}) %collective-permute-start.3) | collective-permute-done | bytes 245792 | tf_op jit(solution)/shard_map/ppermute | solution.py:31
  534.8 0.4 fusion.13
  535.4 0.8 copy.20
  (32 shorter events, 2.3 us)
Async XLA Ops:
  6.5 137.3 %copy-start = (bf16[384,384]{1,0:T(8,128)(2,1)S(1)}, bf16[384,384]{1,0:T(8,128)(2,1)}, u32[]{:S(2)}) copy-start(bf16[384,384]{1,0:T(8,128)(2,1)} %param.11) | copy-start | bytes 884740
  6.5 137.3 %all-gather.8.cloned.1.call-start = ((), (), s32[]{:S(2)}) async-start(), calls=%async_computation.1 | async-start | bytes 4177920 | tf_op jit(solution)/shard_map/all_gather | solution.py:101
  9.9 261.0 %all-gather.10.cloned.1.call-start = ((), (), s32[]{:S(2)}) async-start(), calls=%async_computation.2 | async-start | bytes 4177920 | tf_op jit(solution)/shard_map/all_gather | solution.py:102
  12.2 504.4 %all-gather.6.cloned.1.call-start = ((), (), s32[]{:S(2)}) async-start(), calls=%async_computation | async-start | bytes 8460288 | tf_op jit(solution)/shard_map/all_gather | solution.py:76
  270.9 6.0 %copy-start.1 = (bf16[2,1,160,384]{3,2,1,0:T(8,128)(2,1)S(1)}, bf16[2,1,160,384]{3,2,1,0:T(8,128)(2,1)}, u32[]{:S(2)}) copy-start(bf16[2,1,160,384]{3,2,1,0:T(8,128)(2,1)} %param.9) | copy-start | bytes 737284
  271.0 6.0 %copy-start.3 = (bf16[384,384]{1,0:T(8,128)(2,1)S(1)}, bf16[384,384]{1,0:T(8,128)(2,1)}, u32[]{:S(2)}) copy-start(bf16[384,384]{1,0:T(8,128)(2,1)} %param.14) | copy-start | bytes 884740
  271.0 6.5 %copy-start.4 = (f32[384]{0:T(512)S(1)}, f32[384]{0:T(512)}, u32[]{:S(2)}) copy-start(f32[384]{0:T(512)} %param.15) | copy-start | bytes 4612
  277.6 10.2 %collective-permute-start = (bf16[2,1,160,384]{3,2,0,1:T(8,128)(2,1)S(1)}, bf16[2,1,160,384]{3,2,0,1:T(8,128)(2,1)S(1)}, u32[]{:S(2)}, u32[]{:S(2)}) collective-permute-start(bf16[2,1,160,384]{3,2,0,1:T(8,128)(2,1)S(1)} %multiply_convert_fusion), channel_id=1, source_target_pairs={{0,16},{16,32},{32,48},{48,64},{64,80},{80,96},{96,112},{112,128},... | collective-permute-start | bytes 737288 | tf_op jit(solution)/shard_map/ppermute | solution.py:31
  287.9 13.3 %collective-permute-start.1 = (bf16[4,1,160,384]{3,2,0,1:T(8,128)(2,1)S(1)}, bf16[4,1,160,384]{3,2,0,1:T(8,128)(2,1)S(1)}, u32[]{:S(2)}, u32[]{:S(2)}) collective-permute-start(bf16[4,1,160,384]{3,2,0,1:T(8,128)(2,1)S(1)} %pad_maximum_fusion), channel_id=1, source_target_pairs={{0,1},{1,2},{2,3},{3,4},{4,5},{5,6},{6,7},{7,8},{8,9},{9,10},{10,1... | collective-permute-start | bytes 1474568 | tf_op jit(solution)/shard_map/ppermute | solution.py:19
  292.3 12.0 %collective-permute-start.2 = (bf16[4,1,160,384]{3,2,0,1:T(8,128)(2,1)S(1)}, bf16[4,1,160,384]{3,2,0,1:T(8,128)(2,1)S(1)}, u32[]{:S(2)}, u32[]{:S(2)}) collective-permute-start(bf16[4,1,160,384]{3,2,0,1:T(8,128)(2,1)S(1)} %pad_maximum_fusion), channel_id=1, source_target_pairs={{1,0},{2,1},{3,2},{4,3},{5,4},{6,5},{7,6},{8,7},{9,8},{10,9},{11,1... | collective-permute-start | bytes 1474568 | tf_op jit(solution)/shard_map/ppermute | solution.py:21
  305.3 211.3 %copy-start.5 = (pred[8,21]{0,1:T(8,128)(4,1)S(1)}, pred[8,21]{0,1:T(8,128)(4,1)}, u32[]{:S(2)}) copy-start(pred[8,21]{0,1:T(8,128)(4,1)} %constant.24) | copy-start | bytes 508
  523.7 2.5 copy-start.2
  524.2 10.2 %collective-permute-start.3 = (bf16[2,1,160,384]{3,2,0,1:T(8,128)(2,1)S(1)}, bf16[2,1,160,384]{3,2,0,1:T(8,128)(2,1)S(1)}, u32[]{:S(2)}, u32[]{:S(2)}) collective-permute-start(bf16[2,1,160,384]{3,2,0,1:T(8,128)(2,1)S(1)} %fusion.36), channel_id=1, source_target_pairs={{0,16},{16,32},{32,48},{48,64},{64,80},{80,96},{96,112},{112,128},... | collective-permute-start | bytes 737288 | tf_op jit(solution)/shard_map/ppermute | solution.py:31
Sparse Core Ops, SparseCore 0:
  10.4 133.4 all-gather.7
  146.9 124.0 all-gather.9
  274.0 242.5 all-gather.5
where the time goes:
time: 543 us
  waiting for transfers between devices  488 us (90%)
  matrix products  24.7 us (5%)
  between operations  13.3 us (2%)
  starting transfers between devices  9.79 us (2%)
    all_gather x1, waiting for transfers between devices, rim_conv(): lax.all_gather(conv_weight, 'rows', axis=3, tiled=True)  210 us
    all_gather x1, waiting for transfers between devices, body(): lax.all_gather(key_local, 'rows', axis=1, tiled=True)  131 us
    all_gather x1, waiting for transfers between devices, body(): lax.all_gather(value_local, 'rows', axis=1, tiled=True)  119 us
    ppermute x2, waiting for transfers between devices, shifted(): lax.ppermute(value, axis, [(source, source + steps) for source in range(l...  16.1 us
  transfers between devices with their start and end apart: 7, of which 7 were waited for; matrix products, arithmetic and copies ran while one was open for 4% of the time, Pallas kernels for 0%

commit v1 on v0

v1 whole, which is shorter than its diff:
```python
import math

import jax
import jax.numpy as jnp
from jax import lax
from jax.experimental import pallas as pl
from jax.experimental.pallas import tpu as pltpu
from jax.sharding import PartitionSpec as P

epsilon = 1e-06
MESH = pl.DeviceIdType.MESH
C = 384
W = 160
PART = 256
HALF = 128
PARTS = 8
BLOCK = 672
SCALE = math.log2(math.e) / math.sqrt(C)

PLACE = (0, 2, 3, 1)
STEPS = (
    ((
        ("zo", "part"), ("xo", "part"), ("xo", 1), ("zo", 1), ("X", "part", 0, 3, 0), ("X", "part", 0, 1, 0),
        ("X", "part", 0, 3, 1), ("X", "part", 0, 1, 1), ("X", 1, 0, 3, 0), ("X", 1, 0, 1, 0), ("Z", "part", 3, 0),
        ("Z", "part", 1, 1), ("X", 1, 0, 3, 1), ("X", 1, 0, 1, 1), ("X", "part", 0, 2, 0), ("X", "part", 0, 2, 1),
        ("YO", 0), ("Z", "part", 3, 1), ("Z", "part", 1, 0), ("xo", 0), ("X", 1, 0, 2, 0), ("X", "part", 3, 1, 0),
        ("X", "part", 3, 3, 0), ("X", "part", 1, 1, 1), ("X", "part", 1, 3, 1), ("X", "part", 3, 3, 1),
        ("X", 1, 0, 2, 1),
    ), (
        ("zo", "part"), ("xo", "part"), ("xo", 1), ("X", "part", 0, 3, 0), ("X", "part", 0, 1, 0),
        ("X", "part", 0, 3, 1), ("X", "part", 0, 1, 1), ("X", 1, 0, 3, 0), ("X", 1, 0, 1, 0), ("X", 1, 0, 3, 1),
        ("X", 1, 0, 1, 1), ("X", "part", 0, 2, 0), ("X", "part", 0, 2, 1), ("YO", 0), ("X", 1, 0, 2, 0),
        ("Z", "part", 3, 0), ("Z", "part", 1, 1), ("zo", 1), ("X", 1, 0, 2, 1),
    ), ("pr", 1, 0)),
    ((
        ("X", "part", 1, 3, 0), ("X", "part", 3, 1, 1), ("Y", 0, 3, 0), ("Y", 0, 1, 1), ("X", "part", 1, 1, 0),
        ("X", 0, 0, 3, 0), ("Z", 1, 3, 0), ("Z", 1, 1, 1), ("zo", 0), ("X", 0, 0, 1, 0), ("X", 0, 0, 3, 1),
        ("X", "part", 3, 2, 0), ("Y", 0, 3, 1), ("Y", 0, 1, 0), ("X", 0, 0, 1, 1), ("X", "part", 1, 2, 0),
        ("X", "part", 1, 2, 1), ("YO", 1), ("Z", 1, 3, 1), ("Z", 1, 1, 0), ("X", "part", 3, 2, 1), ("YO", 3),
        ("X", 0, 0, 2, 0), ("Z", "part", 2, 0), ("Z", "part", 2, 1), ("Y", 0, 2, 0), ("Y", 0, 2, 1), ("K", 0),
        ("X", 1, 3, 1, 0), ("X", 1, 3, 3, 0), ("X", 1, 1, 1, 1), ("X", 1, 1, 3, 1), ("X", 0, 0, 2, 1),
        ("Y", 1, 3, 0), ("Y", 1, 1, 1), ("X", 1, 3, 3, 1),
    ), (
        ("Z", "part", 3, 1), ("Z", "part", 1, 0), ("xo", 0), ("X", "part", 3, 3, 0), ("X", "part", 3, 1, 0),
        ("Y", 0, 3, 0), ("Y", 0, 1, 1), ("X", "part", 1, 3, 1), ("X", "part", 1, 1, 1), ("X", "part", 3, 1, 1),
        ("X", "part", 3, 3, 1), ("X", "part", 1, 1, 0), ("X", "part", 1, 3, 0), ("Y", 0, 3, 1), ("Y", 0, 1, 0),
        ("X", 0, 0, 1, 0), ("X", 0, 0, 3, 0), ("X", 0, 0, 1, 1), ("X", 0, 0, 3, 1), ("X", "part", 1, 2, 1),
        ("X", "part", 3, 2, 0), ("Y", 0, 2, 0), ("Y", 0, 2, 1), ("K", 0), ("X", "part", 3, 2, 1), ("YO", 3),
        ("X", "part", 1, 2, 0), ("YO", 1), ("Z", "part", 2, 0), ("Z", "part", 2, 1), ("X", 0, 0, 2, 0),
        ("X", 0, 0, 2, 1),
    ), ("un", 0)),
    ((
        ("X", 1, 3, 1, 1),
    ), (
        ("X", "part", 2, 3, 0), ("X", "part", 2, 1, 0), ("Z", 1, 3, 0), ("Z", 1, 1, 1), ("zo", 0),
        ("X", "part", 2, 3, 1), ("X", "part", 2, 1, 1), ("Y", 3, 3, 0), ("Y", 3, 1, 1),
    ), ("pr", 0, 0)),
    ((
        ("X", 1, 1, 3, 0), ("X", "part", 2, 3, 0), ("X", 1, 1, 1, 0), ("Y", 1, 3, 1), ("Y", 1, 1, 0),
        ("X", "part", 2, 3, 1), ("X", "part", 2, 1, 0), ("X", "part", 2, 1, 1), ("X", 1, 3, 2, 0), ("X", 1, 1, 2, 1),
        ("Y", 3, 3, 0), ("X", 1, 1, 2, 0), ("Y", 3, 1, 1), ("Z", 1, 2, 0), ("Z", 1, 2, 1), ("X", "part", 2, 2, 0),
        ("X", 1, 3, 2, 1),
    ), (
        ("Z", 1, 3, 1), ("Z", 1, 1, 0), ("X", "part", 2, 2, 0), ("X", 1, 3, 1, 0), ("Y", 3, 3, 1), ("Y", 3, 1, 0),
        ("X", 1, 3, 3, 0), ("X", 1, 1, 1, 1), ("X", 1, 1, 3, 1), ("X", "part", 2, 2, 1), ("YO", 2), ("Y", 1, 3, 0),
        ("Y", 1, 1, 1), ("X", 1, 3, 3, 1), ("X", 1, 3, 1, 1), ("X", 1, 1, 3, 0), ("X", 1, 1, 1, 0),
        ("X", 1, 3, 2, 0), ("Y", 1, 3, 1), ("Y", 1, 1, 0), ("X", 1, 1, 2, 1), ("X", 1, 3, 2, 1),
    ), ("pr", 1, 3)),
    ((
        ("X", "part", 2, 2, 1), ("YO", 2),
    ), (
        ("X", 1, 1, 2, 0),
    ), ("pr", 1, 1)),
    ((
        ("Y", 3, 3, 1), ("Y", 3, 1, 0),
    ), (
        ("Y", 3, 2, 0), ("Y", 3, 2, 1), ("K", 3),
    ), ("ask", 1)),
    ((
        ("Z", 0, 3, 0), ("Z", 0, 1, 1), ("X", 1, 2, 3, 0), ("X", 1, 2, 1, 0),
    ), (
        ("Z", 1, 2, 0), ("Z", 1, 2, 1),
    ), ("at", 1, 0)),
    ((
        ("X", 1, 2, 3, 1), ("X", 1, 2, 1, 1), ("Y", 1, 2, 0), ("Y", 1, 2, 1), ("K", 1), ("Z", 0, 3, 1),
        ("Z", 0, 1, 0),
    ), (
        ("Y", 2, 3, 0), ("Y", 2, 1, 1),
    ), ("at", 1, 1)),
    ((
        ("X", 0, 3, 3, 0), ("X", 0, 3, 1, 0), ("X", 0, 1, 3, 1), ("X", 0, 1, 1, 1), ("Y", 3, 2, 0), ("Y", 3, 2, 1),
        ("K", 3), ("X", 1, 2, 2, 0), ("X", 1, 2, 2, 1),
    ), (
        ("Z", 0, 3, 0), ("Z", 0, 1, 1), ("X", 1, 2, 3, 0), ("X", 1, 2, 1, 0), ("X", 1, 2, 3, 1), ("X", 1, 2, 1, 1),
        ("Y", 2, 3, 1), ("Y", 2, 1, 0), ("Z", 0, 3, 1), ("Z", 0, 1, 0), ("X", 0, 3, 3, 0), ("X", 0, 3, 1, 0),
        ("Y", 1, 2, 0), ("Y", 1, 2, 1), ("K", 1), ("X", 0, 1, 3, 1), ("X", 0, 1, 1, 1), ("X", 1, 2, 2, 0),
        ("X", 1, 2, 2, 1),
    ), ("pr", 1, 2)),
    ((
    ), (
        ("Y", 2, 2, 0), ("Y", 2, 2, 1), ("K", 2),
    ), ("at", 1, 2)),
    ((
        ("X", 0, 3, 3, 1), ("X", 0, 3, 1, 1), ("Y", 2, 3, 0), ("Y", 2, 1, 1), ("X", 0, 1, 3, 0), ("X", 0, 1, 1, 0),
    ), (
        ("Z", 0, 2, 0), ("X", 0, 3, 3, 1), ("X", 0, 3, 1, 1), ("Z", 0, 2, 1), ("X", 0, 1, 3, 0), ("X", 0, 1, 1, 0),
    ), ("fin", 1)),
    ((
        ("X", 0, 3, 2, 0), ("X", 0, 1, 2, 1),
    ), (
        ("X", 0, 3, 2, 0), ("X", 0, 1, 2, 1),
    ), ("un", 3)),
    ((
        ("Y", 2, 3, 1), ("Y", 2, 1, 0), ("X", 0, 3, 2, 1),
    ), (
        ("X", 0, 2, 3, 0), ("X", 0, 2, 1, 0), ("X", 0, 2, 3, 1), ("X", 0, 3, 2, 1),
    ), ("pr", 0, 3)),
    ((
        ("X", 0, 1, 2, 0),
    ), (
        ("X", 0, 1, 2, 0),
    ), ("pr", 0, 1)),
    ((
        ("Z", 0, 2, 0), ("Z", 0, 2, 1), ("Y", 2, 2, 0), ("Y", 2, 2, 1), ("K", 2),
    ), (
        ("X", 0, 2, 1, 1),
    ), ("ask", 0)),
    ((
    ), (
        ("X", 0, 2, 2, 0),
    ), ("at", 0, 0)),
    ((
    ), (
    ), ("at", 0, 1)),
    ((
        ("X", 0, 2, 3, 0), ("X", 0, 2, 1, 0), ("X", 0, 2, 3, 1), ("X", 0, 2, 1, 1), ("X", 0, 2, 2, 0),
        ("X", 0, 2, 2, 1),
    ), (
        ("X", 0, 2, 2, 1),
    ), ("pr", 0, 2)),
    ((
    ), (
    ), ("at", 0, 2)),
    ((
    ), (
    ), ("fin", 0)),
    ((
    ), (
    ), ("un", 1)),
    ((
    ), (
    ), ("un", 2)),
    ((
    ), (
    ), ("cv", 0)),
    ((
    ), (
    ), ("cv", 1)),
    ((
    ), (
    ), None),
)


def dot(left, right):
    return jnp.dot(left, right, preferred_element_type=jnp.float32)


def rms_scale(values, gain):
    widened = values.astype(jnp.float32)
    return widened * lax.rsqrt(jnp.mean(widened * widened, axis=-1, keepdims=True) + epsilon) * gain


def kernel(latent_hbm, shard_hbm, attn_gain_hbm, unit_gain_hbm, w_query_hbm, w_key_hbm, w_value_hbm, w_proj_hbm, upsample_hbm, out,
           latent, shard, attn_gain, unit_gain, cells, parts, packed, w_query, w_key_value, w_proj, upsample,
           keys, values, queries, numerator, row_max, attended, extended, conv_weight, sums, units,
           send_sems, grid_sems, y_sems, core_sems, frame_sems, local_sems):
    tm, rows = lax.axis_index("tm"), lax.axis_index("rows")
    z, x = rows // 4, lax.rem(rows, 4)
    core = lax.rem(tm, 2)
    z_lo = lax.rem(tm // 2, 4)
    y = tm // 8

    def ring(value, step):
        return lax.rem(value + (step % 4), 4)

    def to_z(step):
        return {"tm": tm, "rows": ring(z, step) * 4 + x}

    def to_x(step):
        return {"tm": tm, "rows": z * 4 + ring(x, step)}

    def to_y(step):
        return {"tm": (ring(y, step) * 4 + z_lo) * 2 + core, "rows": rows}

    sibling = {"tm": tm + 1 - 2 * core, "rows": rows}
    later = {"tm": lax.rem(tm + 1, 32), "rows": rows}
    before = {"tm": lax.rem(tm + 31, 32), "rows": rows}
    targets = {("z", 1): to_z(1), ("z", -1): to_z(-1), ("x", 1): to_x(1), ("x", -1): to_x(-1),
               ("y", 1): to_y(1), ("y", -1): to_y(-1), ("core", 1): sibling, ("tm", 1): later}

    barrier = pltpu.get_barrier_semaphore()
    greeted = list(targets.values()) + [before]
    for target in greeted:
        pl.semaphore_signal(barrier, inc=1, device_id=target, device_id_type=MESH)

    loads = []
    for source, target in ((shard_hbm, shard), (latent_hbm, latent), (attn_gain_hbm, attn_gain),
                           (unit_gain_hbm, unit_gain), (w_key_hbm, w_key_value.at[:, pl.ds(0, C)]), (w_value_hbm, w_key_value.at[:, pl.ds(C, C)]), (w_query_hbm, w_query),
                           (w_proj_hbm, w_proj), (upsample_hbm, upsample)):
        load = pltpu.make_async_copy(source, target, local_sems.at[2 + len(loads)])
        load.start()
        loads.append(load)
    loads[0].wait()

    for n in range(3):
        packed[pl.ds(BLOCK * n, 640)] = shard[:640, 128 * n:128 * n + 128]
        packed[pl.ds(BLOCK * n + 640, 32)] = jnp.concatenate(
            [shard[640:648, 128 * n:128 * n + 128].astype(jnp.float32), jnp.zeros((24, 128), jnp.float32)],
            axis=0).astype(jnp.bfloat16)
    packed[pl.ds(BLOCK * 3, 32)] = jnp.zeros((32, 128), jnp.bfloat16)

    pl.semaphore_wait(barrier, len(greeted))

    sent = {}

    def slot(dz, dx):
        return ring(z, dz) * 4 + ring(x, dx)

    def cell_unit(frame):
        return lambda dz, dx, h: cells.at[slot(dz, dx), pl.ds(W * frame + W // 2 * h, W // 2)]

    def part_unit(dz, dx, h):
        return parts.at[slot(dz, dx), pl.ds(PART * (core * 4 + y) + HALF * h, HALF)]

    def y_unit(dz, dy, h):
        return parts.at[pl.ds(4 * ring(z, dz), 4), pl.ds(PART * (core * 4 + ring(y, dy)) + HALF * h, HALF)]

    def push(tag, where, parts_of):
        index = sent.setdefault(tag, (len(sent), where, parts_of))[0]
        started(index, where, parts_of).start()

    def started(index, where, parts_of):
        source, target, recv_sem = parts_of()
        return pltpu.make_async_remote_copy(
            src_ref=source, dst_ref=target, send_sem=send_sems.at[index], recv_sem=recv_sem,
            device_id=targets[where], device_id_type=MESH)

    def arrive(region, recv_sem):
        pltpu.make_async_remote_copy(
            src_ref=region, dst_ref=region, send_sem=send_sems.at[0], recv_sem=recv_sem,
            device_id=sibling, device_id_type=MESH).wait_recv()

    grid_kinds = {"part": (part_unit, 0), 0: (cell_unit(0), 32), 1: (cell_unit(1), 64)}

    def grid_sem(kind, dz, dx, h):
        return grid_sems.at[grid_kinds[kind][1] + ((dz % 4) * 4 + dx % 4) * 2 + h]

    def grid_push(kind, dz, dx, h, axis, step, from_own=False):
        def parts_of():
            unit = grid_kinds[kind][0](dz, dx, h)
            sem = grid_sem(kind, dz - step, dx, h) if axis == "z" else grid_sem(kind, dz, dx - step, h)
            return own(kind, h) if from_own else unit, unit, sem

        push((kind, dz, dx, h, axis, step), (axis, step), parts_of)

    def grid_arrive(kind, dz, dx, h):
        arrive(grid_kinds[kind][0](dz, dx, h), grid_sem(kind, dz, dx, h))

    def y_sem(dz, dy, h):
        return y_sems.at[((dz % 4) * 4 + dy % 4) * 2 + h]

    def y_push(dz, dy, h, step):
        push(("y", dz, dy, h, step), ("y", step),
             lambda: (y_unit(dz, dy, h), y_unit(dz, dy, h), y_sem(dz, dy - step, h)))

    def y_arrive(dz, dy, h):
        arrive(y_unit(dz, dy, h), y_sem(dz, dy, h))

    def own(kind, h):
        if kind == "part":
            return packed.at[pl.ds(PART * (core * 4 + y) + HALF * h, HALF)]
        return latent.at[pl.ds(W * kind + W // 2 * h, W // 2)]

    ways = ((0, 1), (1, -1), (1, 1), (0, -1))
    forwarded = {(3, 0): 1, (1, 1): -1}

    def z_own(kind):
        for h, step in ways:
            grid_push(kind, 0, 0, h, "z", step, True)

    def x_out(kind, dz, h, from_own=False):
        first = 1 if h == 0 else -1
        grid_push(kind, dz, 0, h, "x", first, from_own)
        grid_push(kind, dz, 0, h, "x", -first, from_own)

    def x_own(kind):
        for h in range(2):
            x_out(kind, 0, h, True)

    def z_arrival(kind, dz, h):
        grid_arrive(kind, dz, 0, h)
        if (dz, h) in forwarded:
            grid_push(kind, dz, 0, h, "z", forwarded[dz, h])
        x_out(kind, dz, h)

    def x_arrival(kind, dz, dx, h):
        grid_arrive(kind, dz, dx, h)
        if (dx, h) in forwarded:
            grid_push(kind, dz, dx, h, "x", forwarded[dx, h])

    def y_own(dz):
        for h, step in ways:
            y_push(dz, 0, h, step)

    def y_arrival(dz, dy, h):
        y_arrive(dz, dy, h)
        if (dy, h) in forwarded:
            y_push(dz, dy, h, forwarded[dy, h])

    def core_unit(dz, which):
        return parts.at[pl.ds(4 * ring(z, dz), 4), pl.ds(PART * 4 * which, PART * 4)]

    def core_push(dz):
        push(("core", dz), ("core", 1), lambda: (core_unit(dz, core), core_unit(dz, core), core_sems.at[dz % 4]))

    def unpack(dz):
        arrive(core_unit(dz, 1 - core), core_sems.at[dz % 4])
        group = ring(z, dz)
        row = pl.multiple_of(96 * group, 32)

        def taps(loaded, first, count):
            for n in range(3):
                for i in range(3 * count):
                    target = pl.ds(pl.multiple_of(C * (first + i // 3) + row, 32), 96)
                    lanes = slice(C * (i % 3) + 128 * n, C * (i % 3) + 128 * n + 128)
                    conv_weight[target, lanes] = loaded[n][:, i].reshape(96, 128).astype(jnp.bfloat16)

        def load(n, start, count):
            block = parts[pl.ds(4 * group, 4), pl.ds(pl.multiple_of(BLOCK * n + start, 16), count)]
            return block.astype(jnp.float32).reshape(4, count // 24, 24, 128)

        def pair(j, carry):
            taps([load(n, 144 * j, 144) for n in range(3)], 2 * j, 2)
            return carry

        lax.fori_loop(0, 4, pair, 0)
        taps([load(n, 576, 96) for n in range(3)], 8, 1)

    def gained(ref):
        return ref[...].reshape(1, C)

    def project(frame, dz):
        if (frame, dz) == (1, 0):
            for load in loads[2:]:
                load.wait()
        group = ring(z, dz)

        def one(i, carry):
            block = cells[pl.ds(4 * group + 2 * i, 2), pl.ds(W * frame, W)].reshape(2 * W, C)
            normed = rms_scale(block, gained(attn_gain)).astype(jnp.bfloat16)
            place = pl.ds(pl.multiple_of(640 * PLACE[dz] + 2 * W * i, 64), 2 * W)
            both = dot(normed, w_key_value[...]).astype(jnp.bfloat16)
            keys[frame, place] = both[:, :C]
            values[frame, place, 0:C] = both[:, C:]
            return carry

        lax.fori_loop(0, 2, one, 0)

    def ask(frame):
        block = jnp.concatenate([cells[lax.rem(rows + 15 + b, 16), pl.ds(W * frame, W)] for b in range(3)], axis=0)
        normed = rms_scale(block, gained(attn_gain)).astype(jnp.bfloat16)
        queries[frame] = dot(normed, w_query[...]).astype(jnp.bfloat16)

    def attend(h, step):
        asked = (slice(0, 240), slice(240, 480), slice(0, 480))[step]
        place = slice(1920, 2560) if step == 2 else slice(0, 1920)
        scores = lax.dot_general(queries[h, asked], keys[h, place], (((1,), (1,)), ((), ())),
                                 preferred_element_type=jnp.float32)
        top = jnp.max(scores, axis=-1, keepdims=True)
        if step == 2:
            old = row_max[h][:, :1]
            top = jnp.maximum(top, old)
            rescale = jnp.exp2((old - top) * SCALE)
        weights = jnp.exp2((scores - top) * SCALE).astype(jnp.bfloat16)
        added = dot(weights, values[h, place])
        if step == 2:
            numerator[h] = numerator[h] * rescale + added
        else:
            numerator[h, asked] = added
            row_max[h, asked] = jnp.broadcast_to(top, (240, 128))

    def halo_unit(frame, b, half):
        return extended.at[pl.ds(W * frame + W // 2 * half, W // 2), pl.ds(C * b, C)]

    def finish(h):
        scale = 1.0 / numerator[h, :, C:]
        mixed = jnp.concatenate(
            [numerator[h, :, 128 * n:128 * n + 128] * scale for n in range(3)], axis=-1).astype(jnp.bfloat16)
        projected = dot(mixed, w_proj[...])
        for b in range(3):
            here = cells[lax.rem(rows + 15 + b, 16), pl.ds(W * h, W)].astype(jnp.float32)
            summed = (here + projected[W * b:W * b + W]).astype(jnp.bfloat16)
            if b == 1:
                attended[h] = summed
            scaled = rms_scale(summed, gained(unit_gain))
            activated = scaled / (1.0 + jnp.exp(-scaled))
            inside = jnp.logical_and(rows + b >= 1, rows + b <= 16)
            extended[pl.ds(W * (2 + h), W), C * b:C * b + C] = jnp.where(inside, activated, 0.0).astype(jnp.bfloat16)
            for half in range(2):
                push(("halo", h, b, half), ("tm", 1), lambda b=b, half=half: (
                    halo_unit(2 + h, b, half), halo_unit(h, b, half), frame_sems.at[6 * h + 2 * b + half]))

    def earlier(block):
        return jnp.where(tm > 0, block, jnp.zeros_like(block))

    def convolve(a, source, frames):
        block = extended[pl.ds(W * source, W * frames)]
        if source < 2:
            block = earlier(block)
        return dot(block, conv_weight[pl.ds(3 * C * a, 3 * C)])

    def halo(h):
        for b in range(3):
            for half in range(2):
                arrive(halo_unit(h, b, half), frame_sems.at[6 * h + 2 * b + half])

    def early_convolve(number):
        if number == 0:
            sums[pl.ds(W, W)] = convolve(2, 3, 1)
        else:
            halo(1)
            sums[pl.ds(0, W)] = convolve(1, 1, 1)
            sums[pl.ds(W, W)] += convolve(0, 1, 1)

    loads[1].wait()
    own_slice = pl.ds(pl.multiple_of(PART * (core * 4 + y), PART), PART)
    parts[rows, own_slice] = packed[own_slice]
    cells[rows] = latent[...]
    values[:, :, C:] = jnp.ones((2, 2560, 128), jnp.bfloat16)
    actions = {"zo": z_own, "xo": x_own, "Z": z_arrival, "X": x_arrival, "Y": y_arrival, "YO": y_own, "K": core_push,
               "pr": project, "ask": ask, "at": attend, "fin": finish, "un": unpack, "cv": early_convolve}

    def perform(operations):
        for name, *operands in operations:
            actions[name](*operands)

    for ahead, behind, work in STEPS:
        common = 0
        while common < min(len(ahead), len(behind)) and ahead[common] == behind[common]:
            common += 1
        perform(ahead[:common])
        if len(ahead) > common:
            pl.when(z_lo >= 2)(lambda: perform(ahead[common:]))
        if len(behind) > common:
            pl.when(z_lo < 2)(lambda: perform(behind[common:]))
        if work is not None:
            perform((work,))

    column = lax.broadcasted_iota(jnp.int32, (W, C), 0)

    def unit_half(frame, half):
        return units.at[pl.ds(W * frame + W // 2 * half, W // 2)]

    def unit(h, total):
        left = pltpu.roll(total[:, :C], 1, 0)
        right = pltpu.roll(total[:, 2 * C:], W - 1, 0)
        convolved = total[:, C:2 * C] + jnp.where(column > 0, left, 0.0) + jnp.where(column < W - 1, right, 0.0)
        units[pl.ds(W * (2 + h), W)] = (attended[h].astype(jnp.float32) + convolved).astype(jnp.bfloat16)
        for half in range(2):
            push(("unit", h, half), ("tm", 1), lambda half=half: (
                unit_half(2 + h, half), unit_half(h, half), frame_sems.at[12 + 2 * h + half]))

    def earlier_unit(h):
        for half in range(2):
            arrive(unit_half(h, half), frame_sems.at[12 + 2 * h + half])
        return earlier(units[pl.ds(W * h, W)])

    def put(h, stretched):
        out[2 * h] = stretched[:, :C]
        out[2 * h + 1] = stretched[:, C:]

    unit(1, sums[pl.ds(W, W)] + convolve(1, 2, 1))
    sums[pl.ds(0, W)] += convolve(2, 2, 1)
    last = dot(units[pl.ds(W * 3, W)], upsample[2])
    halo(0)
    unit(0, sums[pl.ds(0, W)] + convolve(0, 0, 1))
    newest = units[pl.ds(W * 2, W)]
    last = last + dot(newest, upsample[1])
    first = dot(newest, upsample[2])
    newest = earlier_unit(1)
    put(1, last + dot(newest, upsample[0]))
    first = first + dot(newest, upsample[1])
    put(0, first + dot(earlier_unit(0), upsample[0]))
    for entry in sent.values():
        started(*entry).wait_send()


def body(latent_features, attn_gain, w_query, w_key, w_value, w_proj, unit_gain, conv_weight, upsample_weight):
    vmem = pl.BlockSpec(memory_space=pltpu.VMEM)
    hbm = pl.BlockSpec(memory_space=pltpu.HBM)
    bf16, f32 = jnp.bfloat16, jnp.float32
    out = pl.pallas_call(
        kernel,
        out_shape=jax.ShapeDtypeStruct((4, W, C), f32),
        in_specs=[hbm] * 9,
        out_specs=vmem,
        scratch_shapes=[
            pltpu.VMEM((2 * W, C), bf16),
            pltpu.VMEM((648, C), bf16),
            pltpu.VMEM((C,), f32),
            pltpu.VMEM((C,), f32),
            pltpu.VMEM((16, 2 * W, C), bf16),
            pltpu.VMEM((16, PART * PARTS, 128), bf16),
            pltpu.VMEM((PART * PARTS, 128), bf16),
            pltpu.VMEM((C, C), bf16),
            pltpu.VMEM((C, 2 * C), bf16),
            pltpu.VMEM((C, C), bf16),
            pltpu.VMEM((3, C, 2 * C), bf16),
            pltpu.VMEM((2, 2560, C), bf16),
            pltpu.VMEM((2, 2560, C + 128), bf16),
            pltpu.VMEM((2, 3 * W, C), bf16),
            pltpu.VMEM((2, 3 * W, C + 128), f32),
            pltpu.VMEM((2, 3 * W, 128), f32),
            pltpu.VMEM((2, W, C), bf16),
            pltpu.VMEM((4 * W, 3 * C), bf16),
            pltpu.VMEM((9 * C, 3 * C), bf16),
            pltpu.VMEM((2 * W, 3 * C), f32),
            pltpu.VMEM((4 * W, C), bf16),
            pltpu.SemaphoreType.DMA((136,)),
            pltpu.SemaphoreType.DMA((96,)),
            pltpu.SemaphoreType.DMA((32,)),
            pltpu.SemaphoreType.DMA((4,)),
            pltpu.SemaphoreType.DMA((16,)),
            pltpu.SemaphoreType.DMA((11,)),
        ],
        compiler_params=pltpu.CompilerParams(
            collective_id=0, has_side_effects=True, vmem_limit_bytes=60 * 1024 * 1024),
    )(latent_features.reshape(2 * W, C), conv_weight.reshape(648, C), attn_gain, unit_gain,
      w_query, w_key, w_value, w_proj, upsample_weight)
    return out.astype(bf16).reshape(4, 1, W, C)


def solution(mesh):
    in_specs = (P("tm", "rows", None, None), P(), P(), P(), P(), P(), P(), P(None, None, None, "rows", None), P())
    return jax.shard_map(body, mesh=mesh, in_specs=in_specs, out_specs=P("tm", "rows", None, None), check_vma=False)
```

time: 543 us -> 95.7 us (0.18)
  the two profiles are of different devices: /device:TPU:24 before, /device:TPU:41 now
where the time goes in v1:
time: 95.7 us; the launch traced here: 95.5 us
  Pallas kernels  93.5 us (98%)
  other arithmetic  2.04 us (2%)
    pallas_call x1, Pallas kernels, body(): pl.pallas_call(kernel, out_shape=jax.ShapeDtypeStruct((4, W, C), f32), in...  93.5 us
    reshape x1, other arithmetic, body(): return out.astype(bf16).reshape(4, 1, W, C)  2.04 us

profile of v1, /device:TPU:41, one launch (start us, length us, event | category | flops | bytes accessed | tf_op | source)
XLA Modules:
  0.0 95.5 jit_solution(14933088399698178193)
XLA Ops:
  0.0 93.5 %shard_map.91 = f32[4,160,384]{2,1,0:T(8,128)} custom-call(bf16[320,384]{1,0:T(8,128)(2,1)} %bitcast.7, bf16[648,384]{1,0:T(8,128)(2,1)} %bitcast.6, f32[384]{0:T(512)} %attn_gain_hbm.1, f32[384]{0:T(512)} %unit_gain_hbm.1, bf16[384,384]{1,0:T(8,128)(2,1)} %w_query_hbm.1, bf16[384,384]{1,0:T(8,128)(2,1)} %w_key_hbm.1, bf16[384,384]{1,0:T(8,128)(2,1)} %w_value_hbm.1, ...), custom_call_target="tpu_custom_call" | custom-call | tf_op jit(solution)/shard_map/pallas_call | solution.py:503
  93.5 2.0 %convert_bitcast_fusion = bf16[4,1,160,384]{3,2,1,0:T(8,128)(2,1)} fusion(f32[4,160,384]{2,1,0:T(8,128)} %shard_map.91), kind=kLoop, calls=%fused_computation | loop fusion | flops 245760 | bytes 1474560 | tf_op jit(solution)/shard_map/reshape | solution.py:541

commit v2 on v1

--- a/solution.py
+++ b/solution.py
@@ -37,106 +37,107 @@
         ("X", 0, 0, 3, 0), ("Z", 1, 3, 0), ("Z", 1, 1, 1), ("zo", 0), ("X", 0, 0, 1, 0), ("X", 0, 0, 3, 1),
         ("X", "part", 3, 2, 0), ("Y", 0, 3, 1), ("Y", 0, 1, 0), ("X", 0, 0, 1, 1), ("X", "part", 1, 2, 0),
         ("X", "part", 1, 2, 1), ("YO", 1), ("Z", 1, 3, 1), ("Z", 1, 1, 0), ("X", "part", 3, 2, 1), ("YO", 3),
-        ("X", 0, 0, 2, 0), ("Z", "part", 2, 0), ("Z", "part", 2, 1), ("Y", 0, 2, 0), ("Y", 0, 2, 1), ("K", 0),
+        ("X", 0, 0, 2, 0), ("Z", "part", 2, 0), ("Z", "part", 2, 1), ("Y", 0, 2, 0), ("Y", 0, 2, 1),
         ("X", 1, 3, 1, 0), ("X", 1, 3, 3, 0), ("X", 1, 1, 1, 1), ("X", 1, 1, 3, 1), ("X", 0, 0, 2, 1),
-        ("Y", 1, 3, 0), ("Y", 1, 1, 1), ("X", 1, 3, 3, 1),
+        ("Y", 1, 3, 0), ("Y", 1, 1, 1), ("X", 1, 3, 3, 1), ("X", 1, 3, 1, 1), ("X", 1, 1, 3, 0),
+        ("X", "part", 2, 3, 0), ("X", 1, 1, 1, 0), ("Y", 1, 3, 1), ("Y", 1, 1, 0), ("X", "part", 2, 3, 1),
+        ("X", "part", 2, 1, 0), ("X", "part", 2, 1, 1), ("X", 1, 3, 2, 0), ("X", 1, 1, 2, 1), ("Y", 3, 3, 0),
+        ("X", 1, 1, 2, 0), ("Y", 3, 1, 1),
     ), (
         ("Z", "part", 3, 1), ("Z", "part", 1, 0), ("xo", 0), ("X", "part", 3, 3, 0), ("X", "part", 3, 1, 0),
         ("Y", 0, 3, 0), ("Y", 0, 1, 1), ("X", "part", 1, 3, 1), ("X", "part", 1, 1, 1), ("X", "part", 3, 1, 1),
         ("X", "part", 3, 3, 1), ("X", "part", 1, 1, 0), ("X", "part", 1, 3, 0), ("Y", 0, 3, 1), ("Y", 0, 1, 0),
         ("X", 0, 0, 1, 0), ("X", 0, 0, 3, 0), ("X", 0, 0, 1, 1), ("X", 0, 0, 3, 1), ("X", "part", 1, 2, 1),
-        ("X", "part", 3, 2, 0), ("Y", 0, 2, 0), ("Y", 0, 2, 1), ("K", 0), ("X", "part", 3, 2, 1), ("YO", 3),
+        ("X", "part", 3, 2, 0), ("Y", 0, 2, 0), ("Y", 0, 2, 1), ("X", "part", 3, 2, 1), ("YO", 3),
         ("X", "part", 1, 2, 0), ("YO", 1), ("Z", "part", 2, 0), ("Z", "part", 2, 1), ("X", 0, 0, 2, 0),
-        ("X", 0, 0, 2, 1),
+        ("X", 0, 0, 2, 1), ("X", "part", 2, 3, 0), ("Z", 1, 3, 0), ("X", "part", 2, 1, 0), ("Z", 1, 1, 1), ("zo", 0),
+        ("X", "part", 2, 3, 1), ("X", "part", 2, 1, 1),
     ), ("un", 0)),
     ((
-        ("X", 1, 3, 1, 1),
-    ), (
-        ("X", "part", 2, 3, 0), ("X", "part", 2, 1, 0), ("Z", 1, 3, 0), ("Z", 1, 1, 1), ("zo", 0),
-        ("X", "part", 2, 3, 1), ("X", "part", 2, 1, 1), ("Y", 3, 3, 0), ("Y", 3, 1, 1),
+        ("Z", 1, 2, 0), ("Z", 1, 2, 1), ("X", "part", 2, 2, 0), ("X", 1, 3, 2, 1),
+    ), (
+        ("Y", 3, 3, 0), ("Y", 3, 1, 1),
     ), ("pr", 0, 0)),
     ((
-        ("X", 1, 1, 3, 0), ("X", "part", 2, 3, 0), ("X", 1, 1, 1, 0), ("Y", 1, 3, 1), ("Y", 1, 1, 0),
-        ("X", "part", 2, 3, 1), ("X", "part", 2, 1, 0), ("X", "part", 2, 1, 1), ("X", 1, 3, 2, 0), ("X", 1, 1, 2, 1),
-        ("Y", 3, 3, 0), ("X", 1, 1, 2, 0), ("Y", 3, 1, 1), ("Z", 1, 2, 0), ("Z", 1, 2, 1), ("X", "part", 2, 2, 0),
-        ("X", 1, 3, 2, 1),
-    ), (
-        ("Z", 1, 3, 1), ("Z", 1, 1, 0), ("X", "part", 2, 2, 0), ("X", 1, 3, 1, 0), ("Y", 3, 3, 1), ("Y", 3, 1, 0),
-        ("X", 1, 3, 3, 0), ("X", 1, 1, 1, 1), ("X", 1, 1, 3, 1), ("X", "part", 2, 2, 1), ("YO", 2), ("Y", 1, 3, 0),
-        ("Y", 1, 1, 1), ("X", 1, 3, 3, 1), ("X", 1, 3, 1, 1), ("X", 1, 1, 3, 0), ("X", 1, 1, 1, 0),
-        ("X", 1, 3, 2, 0), ("Y", 1, 3, 1), ("Y", 1, 1, 0), ("X", 1, 1, 2, 1), ("X", 1, 3, 2, 1),
+        ("X", "part", 2, 2, 1), ("YO", 2), ("Y", 3, 3, 1), ("Y", 3, 1, 0),
+    ), (
+        ("X", "part", 2, 2, 0), ("Z", 1, 3, 1), ("Z", 1, 1, 0), ("X", 1, 3, 1, 0), ("X", 1, 3, 3, 0), ("Y", 3, 3, 1),
+        ("Y", 3, 1, 0), ("X", 1, 1, 1, 1), ("X", 1, 1, 3, 1), ("X", "part", 2, 2, 1), ("YO", 2), ("X", 1, 3, 3, 1),
+        ("X", 1, 3, 1, 1), ("Y", 1, 3, 0), ("Y", 1, 1, 1), ("X", 1, 1, 3, 0), ("X", 1, 1, 1, 0), ("X", 1, 3, 2, 0),
+        ("X", 1, 1, 2, 1), ("Y", 1, 3, 1), ("Y", 1, 1, 0), ("X", 1, 3, 2, 1),
     ), ("pr", 1, 3)),
     ((
-        ("X", "part", 2, 2, 1), ("YO", 2),
+        ("Z", 0, 3, 0), ("Z", 0, 1, 1),
     ), (
         ("X", 1, 1, 2, 0),
     ), ("pr", 1, 1)),
     ((
-        ("Y", 3, 3, 1), ("Y", 3, 1, 0),
-    ), (
-        ("Y", 3, 2, 0), ("Y", 3, 2, 1), ("K", 3),
+        ("X", 1, 2, 3, 0), ("X", 1, 2, 1, 0),
+    ), (
     ), ("ask", 1)),
     ((
-        ("Z", 0, 3, 0), ("Z", 0, 1, 1), ("X", 1, 2, 3, 0), ("X", 1, 2, 1, 0),
+        ("Y", 1, 2, 0), ("Y", 1, 2, 1), ("Z", 0, 3, 1), ("X", 1, 2, 3, 1), ("Z", 0, 1, 0), ("X", 1, 2, 1, 1),
+    ), (
+        ("Y", 3, 2, 0), ("Y", 3, 2, 1),
+    ), ("at", 1, 0)),
+    ((
+        ("X", 0, 3, 3, 0), ("X", 0, 3, 1, 0),
     ), (
         ("Z", 1, 2, 0), ("Z", 1, 2, 1),
-    ), ("at", 1, 0)),
-    ((
-        ("X", 1, 2, 3, 1), ("X", 1, 2, 1, 1), ("Y", 1, 2, 0), ("Y", 1, 2, 1), ("K", 1), ("Z", 0, 3, 1),
-        ("Z", 0, 1, 0),
-    ), (
-        ("Y", 2, 3, 0), ("Y", 2, 1, 1),
     ), ("at", 1, 1)),
     ((
-        ("X", 0, 3, 3, 0), ("X", 0, 3, 1, 0), ("X", 0, 1, 3, 1), ("X", 0, 1, 1, 1), ("Y", 3, 2, 0), ("Y", 3, 2, 1),
-        ("K", 3), ("X", 1, 2, 2, 0), ("X", 1, 2, 2, 1),
-    ), (
-        ("Z", 0, 3, 0), ("Z", 0, 1, 1), ("X", 1, 2, 3, 0), ("X", 1, 2, 1, 0), ("X", 1, 2, 3, 1), ("X", 1, 2, 1, 1),
-        ("Y", 2, 3, 1), ("Y", 2, 1, 0), ("Z", 0, 3, 1), ("Z", 0, 1, 0), ("X", 0, 3, 3, 0), ("X", 0, 3, 1, 0),
-        ("Y", 1, 2, 0), ("Y", 1, 2, 1), ("K", 1), ("X", 0, 1, 3, 1), ("X", 0, 1, 1, 1), ("X", 1, 2, 2, 0),
-        ("X", 1, 2, 2, 1),
+        ("X", 0, 1, 3, 1), ("Y", 3, 2, 0), ("X", 0, 1, 1, 1), ("Y", 3, 2, 1), ("X", 1, 2, 2, 0), ("X", 0, 3, 1, 1),
+        ("X", 0, 3, 3, 1), ("X", 0, 1, 1, 0), ("Y", 2, 3, 0), ("Y", 2, 1, 1), ("X", 0, 1, 3, 0), ("X", 1, 2, 2, 1),
+    ), (
+        ("Y", 2, 3, 0), ("Y", 2, 1, 1), ("Z", 0, 3, 0), ("Z", 0, 1, 1), ("X", 1, 2, 3, 0), ("X", 1, 2, 1, 0),
+        ("Y", 2, 3, 1), ("Y", 2, 1, 0), ("Z", 0, 3, 1), ("Z", 0, 1, 0), ("X", 1, 2, 3, 1), ("X", 1, 2, 1, 1),
+        ("X", 0, 3, 3, 0), ("X", 0, 3, 1, 0), ("Y", 1, 2, 0), ("Y", 1, 2, 1), ("X", 0, 1, 3, 1), ("X", 0, 1, 1, 1),
+        ("X", 1, 2, 2, 0), ("X", 0, 3, 1, 1), ("Y", 2, 2, 0), ("Z", 0, 2, 0), ("Y", 2, 2, 1), ("Z", 0, 2, 1),
+        ("X", 0, 3, 3, 1), ("X", 0, 1, 1, 0), ("X", 0, 1, 3, 0), ("X", 1, 2, 2, 1),
     ), ("pr", 1, 2)),
     ((
     ), (
-        ("Y", 2, 2, 0), ("Y", 2, 2, 1), ("K", 2),
     ), ("at", 1, 2)),
     ((
-        ("X", 0, 3, 3, 1), ("X", 0, 3, 1, 1), ("Y", 2, 3, 0), ("Y", 2, 1, 1), ("X", 0, 1, 3, 0), ("X", 0, 1, 1, 0),
-    ), (
-        ("Z", 0, 2, 0), ("X", 0, 3, 3, 1), ("X", 0, 3, 1, 1), ("Z", 0, 2, 1), ("X", 0, 1, 3, 0), ("X", 0, 1, 1, 0),
+        ("X", 0, 3, 2, 0), ("X", 0, 1, 2, 1), ("Y", 2, 3, 1), ("Y", 2, 1, 0), ("X", 0, 3, 2, 1),
+    ), (
+        ("X", 0, 3, 2, 0), ("X", 0, 1, 2, 1),
     ), ("fin", 1)),
     ((
-        ("X", 0, 3, 2, 0), ("X", 0, 1, 2, 1),
-    ), (
-        ("X", 0, 3, 2, 0), ("X", 0, 1, 2, 1),
+        ("X", 0, 1, 2, 0), ("Z", 0, 2, 0), ("Z", 0, 2, 1), ("Y", 2, 2, 0), ("Y", 2, 2, 1),
+    ), (
+        ("X", 0, 2, 3, 0), ("X", 0, 3, 2, 1), ("X", 0, 2, 3, 1), ("X", 0, 2, 1, 0),
     ), ("un", 3)),
     ((
-        ("Y", 2, 3, 1), ("Y", 2, 1, 0), ("X", 0, 3, 2, 1),
-    ), (
-        ("X", 0, 2, 3, 0), ("X", 0, 2, 1, 0), ("X", 0, 2, 3, 1), ("X", 0, 3, 2, 1),
+    ), (
+        ("X", 0, 1, 2, 0), ("X", 0, 2, 1, 1),
     ), ("pr", 0, 3)),
     ((
-        ("X", 0, 1, 2, 0),
-    ), (
-        ("X", 0, 1, 2, 0),
+    ), (
     ), ("pr", 0, 1)),
     ((
-        ("Z", 0, 2, 0), ("Z", 0, 2, 1), ("Y", 2, 2, 0), ("Y", 2, 2, 1), ("K", 2),
-    ), (
-        ("X", 0, 2, 1, 1),
+        ("X", 0, 2, 3, 0), ("X", 0, 2, 1, 0),
+    ), (
     ), ("ask", 0)),
     ((
+        ("X", 0, 2, 3, 1), ("X", 0, 2, 1, 1),
     ), (
         ("X", 0, 2, 2, 0),
     ), ("at", 0, 0)),
     ((
     ), (
+        ("X", 0, 2, 2, 1),
+    ), ("un", 1)),
+    ((
+        ("X", 0, 2, 2, 0),
+    ), (
     ), ("at", 0, 1)),
     ((
-        ("X", 0, 2, 3, 0), ("X", 0, 2, 1, 0), ("X", 0, 2, 3, 1), ("X", 0, 2, 1, 1), ("X", 0, 2, 2, 0),
         ("X", 0, 2, 2, 1),
     ), (
-        ("X", 0, 2, 2, 1),
+    ), ("un", 2)),
+    ((
+    ), (
     ), ("pr", 0, 2)),
     ((
     ), (
@@ -144,18 +145,6 @@
     ((
     ), (
     ), ("fin", 0)),
-    ((
-    ), (
-    ), ("un", 1)),
-    ((
-    ), (
-    ), ("un", 2)),
-    ((
-    ), (
-    ), ("cv", 0)),
-    ((
-    ), (
-    ), ("cv", 1)),
     ((
     ), (
     ), None),
@@ -173,7 +162,7 @@
 
 def kernel(latent_hbm, shard_hbm, attn_gain_hbm, unit_gain_hbm, w_query_hbm, w_key_hbm, w_value_hbm, w_proj_hbm, upsample_hbm, out,
            latent, shard, attn_gain, unit_gain, cells, parts, packed, w_query, w_key_value, w_proj, upsample,
-           keys, values, queries, numerator, row_max, attended, extended, conv_weight, sums, units,
+           keys, values, queries, numerator, row_max, attended, extended, conv_weight, sums, units, carried,
            send_sems, grid_sems, y_sems, core_sems, frame_sems, local_sems):
     tm, rows = lax.axis_index("tm"), lax.axis_index("rows")
     z, x = rows // 4, lax.rem(rows, 4)
@@ -312,20 +301,29 @@
     def y_own(dz):
         for h, step in ways:
             y_push(dz, 0, h, step)
+        for h in range(2):
+            core_push(dz, 0, h)
 
     def y_arrival(dz, dy, h):
         y_arrive(dz, dy, h)
         if (dy, h) in forwarded:
             y_push(dz, dy, h, forwarded[dy, h])
-
-    def core_unit(dz, which):
-        return parts.at[pl.ds(4 * ring(z, dz), 4), pl.ds(PART * 4 * which, PART * 4)]
-
-    def core_push(dz):
-        push(("core", dz), ("core", 1), lambda: (core_unit(dz, core), core_unit(dz, core), core_sems.at[dz % 4]))
+        core_push(dz, dy, h)
+
+    def core_unit(dz, dy, h, which):
+        return parts.at[pl.ds(4 * ring(z, dz), 4), pl.ds(PART * (which * 4 + ring(y, dy)) + HALF * h, HALF)]
+
+    def core_sem(dz, dy, h):
+        return core_sems.at[((dz % 4) * 4 + dy % 4) * 2 + h]
+
+    def core_push(dz, dy, h):
+        push(("core", dz, dy, h), ("core", 1),
+             lambda: (core_unit(dz, dy, h, core), core_unit(dz, dy, h, core), core_sem(dz, dy, h)))
 
     def unpack(dz):
-        arrive(core_unit(dz, 1 - core), core_sems.at[dz % 4])
+        for dy in range(4):
+            for h in range(2):
+                arrive(core_unit(dz, dy, h, 1 - core), core_sem(dz, dy, h))
         group = ring(z, dz)
         row = pl.multiple_of(96 * group, 32)
 
@@ -407,7 +405,7 @@
             activated = scaled / (1.0 + jnp.exp(-scaled))
             inside = jnp.logical_and(rows + b >= 1, rows + b <= 16)
             extended[pl.ds(W * (2 + h), W), C * b:C * b + C] = jnp.where(inside, activated, 0.0).astype(jnp.bfloat16)
-            for half in range(2):
+            for half in range(2 * h):
                 push(("halo", h, b, half), ("tm", 1), lambda b=b, half=half: (
                     halo_unit(2 + h, b, half), halo_unit(h, b, half), frame_sems.at[6 * h + 2 * b + half]))
 
@@ -420,26 +418,28 @@
             block = earlier(block)
         return dot(block, conv_weight[pl.ds(3 * C * a, 3 * C)])
 
-    def halo(h):
+    def halo():
         for b in range(3):
             for half in range(2):
-                arrive(halo_unit(h, b, half), frame_sems.at[6 * h + 2 * b + half])
-
-    def early_convolve(number):
-        if number == 0:
-            sums[pl.ds(W, W)] = convolve(2, 3, 1)
-        else:
-            halo(1)
-            sums[pl.ds(0, W)] = convolve(1, 1, 1)
-            sums[pl.ds(W, W)] += convolve(0, 1, 1)
+                arrive(halo_unit(1, b, half), frame_sems.at[6 + 2 * b + half])
+
+    column = lax.broadcasted_iota(jnp.int32, (W, C), 0)
+
+    def joined(total):
+        left = pltpu.roll(total[:, :C], 1, 0)
+        right = pltpu.roll(total[:, 2 * C:], W - 1, 0)
+        return total[:, C:2 * C] + jnp.where(column > 0, left, 0.0) + jnp.where(column < W - 1, right, 0.0)
+
+    def carried_half(place, half):
+        return carried.at[pl.ds(W * place + W // 2 * half, W // 2)]
 
     loads[1].wait()
     own_slice = pl.ds(pl.multiple_of(PART * (core * 4 + y), PART), PART)
     parts[rows, own_slice] = packed[own_slice]
     cells[rows] = latent[...]
     values[:, :, C:] = jnp.ones((2, 2560, 128), jnp.bfloat16)
-    actions = {"zo": z_own, "xo": x_own, "Z": z_arrival, "X": x_arrival, "Y": y_arrival, "YO": y_own, "K": core_push,
-               "pr": project, "ask": ask, "at": attend, "fin": finish, "un": unpack, "cv": early_convolve}
+    actions = {"zo": z_own, "xo": x_own, "Z": z_arrival, "X": x_arrival, "Y": y_arrival, "YO": y_own,
+               "pr": project, "ask": ask, "at": attend, "fin": finish, "un": unpack}
 
     def perform(operations):
         for name, *operands in operations:
@@ -457,15 +457,15 @@
         if work is not None:
             perform((work,))
 
-    column = lax.broadcasted_iota(jnp.int32, (W, C), 0)
+    carried[pl.ds(W, W)] = joined(convolve(0, 2, 1)).astype(jnp.bfloat16)
+    for half in range(2):
+        push(("carried", half), ("tm", 1), lambda half=half: (
+            carried_half(1, half), carried_half(0, half), frame_sems.at[half]))
 
     def unit_half(frame, half):
         return units.at[pl.ds(W * frame + W // 2 * half, W // 2)]
 
-    def unit(h, total):
-        left = pltpu.roll(total[:, :C], 1, 0)
-        right = pltpu.roll(total[:, 2 * C:], W - 1, 0)
-        convolved = total[:, C:2 * C] + jnp.where(column > 0, left, 0.0) + jnp.where(column < W - 1, right, 0.0)
+    def unit(h, convolved):
         units[pl.ds(W * (2 + h), W)] = (attended[h].astype(jnp.float32) + convolved).astype(jnp.bfloat16)
         for half in range(2):
             push(("unit", h, half), ("tm", 1), lambda half=half: (
@@ -480,11 +480,15 @@
         out[2 * h] = stretched[:, :C]
         out[2 * h + 1] = stretched[:, C:]
 
-    unit(1, sums[pl.ds(W, W)] + convolve(1, 2, 1))
-    sums[pl.ds(0, W)] += convolve(2, 2, 1)
+    sums[...] = convolve(2, 2, 2)
+    sums[pl.ds(W, W)] += convolve(1, 2, 1)
+    halo()
+    unit(1, joined(sums[pl.ds(W, W)] + convolve(0, 1, 1)))
+    convolved = joined(sums[pl.ds(0, W)] + convolve(1, 1, 1))
     last = dot(units[pl.ds(W * 3, W)], upsample[2])
-    halo(0)
-    unit(0, sums[pl.ds(0, W)] + convolve(0, 0, 1))
+    for half in range(2):
+        arrive(carried_half(0, half), frame_sems.at[half])
+    unit(0, convolved + earlier(carried[pl.ds(0, W)]).astype(jnp.float32))
     newest = units[pl.ds(W * 2, W)]
     last = last + dot(newest, upsample[1])
     first = dot(newest, upsample[2])
@@ -527,10 +531,11 @@
             pltpu.VMEM((9 * C, 3 * C), bf16),
             pltpu.VMEM((2 * W, 3 * C), f32),
             pltpu.VMEM((4 * W, C), bf16),
-            pltpu.SemaphoreType.DMA((136,)),
+            pltpu.VMEM((2 * W, C), bf16),
+            pltpu.SemaphoreType.DMA((162,)),
             pltpu.SemaphoreType.DMA((96,)),
             pltpu.SemaphoreType.DMA((32,)),
-            pltpu.SemaphoreType.DMA((4,)),
+            pltpu.SemaphoreType.DMA((32,)),
             pltpu.SemaphoreType.DMA((16,)),
             pltpu.SemaphoreType.DMA((11,)),
         ],

time: 95.7 us -> 96.2 us (level)
  the two profiles are of different devices: /device:TPU:41 before, /device:TPU:24 now
where the time goes in v2:
time: 96.2 us; the launch traced here: 95.2 us
  Pallas kernels  93.1 us (97%)
  other arithmetic  2.04 us (2%)
    pallas_call x1, Pallas kernels, body(): pl.pallas_call(kernel, out_shape=jax.ShapeDtypeStruct((4, W, C), f32), in...  93.1 us
    reshape x1, other arithmetic, body(): return out.astype(bf16).reshape(4, 1, W, C)  2.04 us

profile of v2, /device:TPU:24, one launch (start us, length us, event | category | flops | bytes accessed | tf_op | source)
XLA Modules:
  0.0 95.2 jit_solution(7487486234371947357)
XLA Ops:
  0.0 93.1 %shard_map.91 = f32[4,160,384]{2,1,0:T(8,128)} custom-call(bf16[320,384]{1,0:T(8,128)(2,1)} %bitcast.7, bf16[648,384]{1,0:T(8,128)(2,1)} %bitcast.6, f32[384]{0:T(512)} %attn_gain_hbm.1, f32[384]{0:T(512)} %unit_gain_hbm.1, bf16[384,384]{1,0:T(8,128)(2,1)} %w_query_hbm.1, bf16[384,384]{1,0:T(8,128)(2,1)} %w_key_hbm.1, bf16[384,384]{1,0:T(8,128)(2,1)} %w_value_hbm.1, ...), custom_call_target="tpu_custom_call" | custom-call | tf_op jit(solution)/shard_map/pallas_call | solution.py:507
  93.1 2.0 %convert_bitcast_fusion = bf16[4,1,160,384]{3,2,1,0:T(8,128)(2,1)} fusion(f32[4,160,384]{2,1,0:T(8,128)} %shard_map.91), kind=kLoop, calls=%fused_computation | loop fusion | flops 245760 | bytes 1474560 | tf_op jit(solution)/shard_map/reshape | solution.py:546

commit v3 on v2

--- a/solution.py
+++ b/solution.py
@@ -136,6 +136,9 @@
         ("X", 0, 2, 2, 1),
     ), (
     ), ("un", 2)),
+    ((
+    ), (
+    ), ("cv", 0)),
     ((
     ), (
     ), ("pr", 0, 2)),
@@ -388,9 +391,6 @@
             numerator[h, asked] = added
             row_max[h, asked] = jnp.broadcast_to(top, (240, 128))
 
-    def halo_unit(frame, b, half):
-        return extended.at[pl.ds(W * frame + W // 2 * half, W // 2), pl.ds(C * b, C)]
-
     def finish(h):
         scale = 1.0 / numerator[h, :, C:]
         mixed = jnp.concatenate(
@@ -404,24 +404,13 @@
             scaled = rms_scale(summed, gained(unit_gain))
             activated = scaled / (1.0 + jnp.exp(-scaled))
             inside = jnp.logical_and(rows + b >= 1, rows + b <= 16)
-            extended[pl.ds(W * (2 + h), W), C * b:C * b + C] = jnp.where(inside, activated, 0.0).astype(jnp.bfloat16)
-            for half in range(2 * h):
-                push(("halo", h, b, half), ("tm", 1), lambda b=b, half=half: (
-                    halo_unit(2 + h, b, half), halo_unit(h, b, half), frame_sems.at[6 * h + 2 * b + half]))
+            extended[pl.ds(W * h, W), C * b:C * b + C] = jnp.where(inside, activated, 0.0).astype(jnp.bfloat16)
 
     def earlier(block):
         return jnp.where(tm > 0, block, jnp.zeros_like(block))
 
     def convolve(a, source, frames):
-        block = extended[pl.ds(W * source, W * frames)]
-        if source < 2:
-            block = earlier(block)
-        return dot(block, conv_weight[pl.ds(3 * C * a, 3 * C)])
-
-    def halo():
-        for b in range(3):
-            for half in range(2):
-                arrive(halo_unit(1, b, half), frame_sems.at[6 + 2 * b + half])
+        return dot(extended[pl.ds(W * (source - 2), W * frames)], conv_weight[pl.ds(3 * C * a, 3 * C)])
 
     column = lax.broadcasted_iota(jnp.int32, (W, C), 0)
 
@@ -432,6 +421,21 @@
 
     def carried_half(place, half):
         return carried.at[pl.ds(W * place + W // 2 * half, W // 2)]
+
+    def carry(h, total):
+        carried[pl.ds(W * (2 + h), W)] = joined(total).astype(jnp.bfloat16)
+        for half in range(2):
+            push(("carried", h, half), ("tm", 1), lambda half=half: (
+                carried_half(2 + h, half), carried_half(h, half), frame_sems.at[2 * h + half]))
+
+    def brought(h):
+        for half in range(2):
+            arrive(carried_half(h, half), frame_sems.at[2 * h + half])
+        return earlier(carried[pl.ds(W * h, W)]).astype(jnp.float32)
+
+    def early_convolve(number):
+        sums[pl.ds(0, W)] = convolve(1, 3, 1)
+        carry(1, convolve(0, 3, 1))
 
     loads[1].wait()
     own_slice = pl.ds(pl.multiple_of(PART * (core * 4 + y), PART), PART)
@@ -439,7 +443,7 @@
     cells[rows] = latent[...]
     values[:, :, C:] = jnp.ones((2, 2560, 128), jnp.bfloat16)
     actions = {"zo": z_own, "xo": x_own, "Z": z_arrival, "X": x_arrival, "Y": y_arrival, "YO": y_own,
-               "pr": project, "ask": ask, "at": attend, "fin": finish, "un": unpack}
+               "pr": project, "ask": ask, "at": attend, "fin": finish, "un": unpack, "cv": early_convolve}
 
     def perform(operations):
         for name, *operands in operations:
@@ -451,16 +455,13 @@
             common += 1
         perform(ahead[:common])
         if len(ahead) > common:
-            pl.when(z_lo >= 2)(lambda: perform(ahead[common:]))
+            pl.when(z_lo == 3)(lambda: perform(ahead[common:]))
         if len(behind) > common:
-            pl.when(z_lo < 2)(lambda: perform(behind[common:]))
+            pl.when(z_lo < 3)(lambda: perform(behind[common:]))
         if work is not None:
             perform((work,))
 
-    carried[pl.ds(W, W)] = joined(convolve(0, 2, 1)).astype(jnp.bfloat16)
-    for half in range(2):
-        push(("carried", half), ("tm", 1), lambda half=half: (
-            carried_half(1, half), carried_half(0, half), frame_sems.at[half]))
+    carry(0, sums[pl.ds(0, W)] + convolve(0, 2, 1))
 
     def unit_half(frame, half):
         return units.at[pl.ds(W * frame + W // 2 * half, W // 2)]
@@ -469,11 +470,11 @@
         units[pl.ds(W * (2 + h), W)] = (attended[h].astype(jnp.float32) + convolved).astype(jnp.bfloat16)
         for half in range(2):
             push(("unit", h, half), ("tm", 1), lambda half=half: (
-                unit_half(2 + h, half), unit_half(h, half), frame_sems.at[12 + 2 * h + half]))
+                unit_half(2 + h, half), unit_half(h, half), frame_sems.at[4 + 2 * h + half]))
 
     def earlier_unit(h):
         for half in range(2):
-            arrive(unit_half(h, half), frame_sems.at[12 + 2 * h + half])
+            arrive(unit_half(h, half), frame_sems.at[4 + 2 * h + half])
         return earlier(units[pl.ds(W * h, W)])
 
     def put(h, stretched):
@@ -482,13 +483,10 @@
 
     sums[...] = convolve(2, 2, 2)
     sums[pl.ds(W, W)] += convolve(1, 2, 1)
-    halo()
-    unit(1, joined(sums[pl.ds(W, W)] + convolve(0, 1, 1)))
-    convolved = joined(sums[pl.ds(0, W)] + convolve(1, 1, 1))
+    unit(1, joined(sums[pl.ds(W, W)]) + brought(1))
+    convolved = joined(sums[pl.ds(0, W)])
     last = dot(units[pl.ds(W * 3, W)], upsample[2])
-    for half in range(2):
-        arrive(carried_half(0, half), frame_sems.at[half])
-    unit(0, convolved + earlier(carried[pl.ds(0, W)]).astype(jnp.float32))
+    unit(0, convolved + brought(0))
     newest = units[pl.ds(W * 2, W)]
     last = last + dot(newest, upsample[1])
     first = dot(newest, upsample[2])
@@ -527,16 +525,16 @@
             pltpu.VMEM((2, 3 * W, C + 128), f32),
             pltpu.VMEM((2, 3 * W, 128), f32),
             pltpu.VMEM((2, W, C), bf16),
-            pltpu.VMEM((4 * W, 3 * C), bf16),
+            pltpu.VMEM((2 * W, 3 * C), bf16),
             pltpu.VMEM((9 * C, 3 * C), bf16),
             pltpu.VMEM((2 * W, 3 * C), f32),
             pltpu.VMEM((4 * W, C), bf16),
-            pltpu.VMEM((2 * W, C), bf16),
-            pltpu.SemaphoreType.DMA((162,)),
+            pltpu.VMEM((4 * W, C), bf16),
+            pltpu.SemaphoreType.DMA((154,)),
             pltpu.SemaphoreType.DMA((96,)),
             pltpu.SemaphoreType.DMA((32,)),
             pltpu.SemaphoreType.DMA((32,)),
-            pltpu.SemaphoreType.DMA((16,)),
+            pltpu.SemaphoreType.DMA((8,)),
             pltpu.SemaphoreType.DMA((11,)),
         ],
         compiler_params=pltpu.CompilerParams(

time: 96.2 us -> 91.8 us (0.954)
  Pallas kernels: 93.1 us -> 88 us
    pallas_call x1, Pallas kernels: 93.1 us -> 88 us  [body(): pl.pallas_call(kernel, out_shape=jax.ShapeDtypeStruct((4, W, C), f32), in...]
where the time goes in v3:
time: 91.8 us; the launch traced here: 90 us
  Pallas kernels  88 us (96%)
  other arithmetic  2.04 us (2%)
    pallas_call x1, Pallas kernels, body(): pl.pallas_call(kernel, out_shape=jax.ShapeDtypeStruct((4, W, C), f32), in...  88 us
    reshape x1, other arithmetic, body(): return out.astype(bf16).reshape(4, 1, W, C)  2.04 us

profile of v3, /device:TPU:24, one launch (start us, length us, event | category | flops | bytes accessed | tf_op | source)
XLA Modules:
  0.0 90.0 jit_solution(3751365236470318975)
XLA Ops:
  0.0 88.0 %shard_map.91 = f32[4,160,384]{2,1,0:T(8,128)} custom-call(bf16[320,384]{1,0:T(8,128)(2,1)} %bitcast.7, bf16[648,384]{1,0:T(8,128)(2,1)} %bitcast.6, f32[384]{0:T(512)} %attn_gain_hbm.1, f32[384]{0:T(512)} %unit_gain_hbm.1, bf16[384,384]{1,0:T(8,128)(2,1)} %w_query_hbm.1, bf16[384,384]{1,0:T(8,128)(2,1)} %w_key_hbm.1, bf16[384,384]{1,0:T(8,128)(2,1)} %w_value_hbm.1, ...), custom_call_target="tpu_custom_call" | custom-call | tf_op jit(solution)/shard_map/pallas_call | solution.py:505
  88.0 2.0 %convert_bitcast_fusion = bf16[4,1,160,384]{3,2,1,0:T(8,128)(2,1)} fusion(f32[4,160,384]{2,1,0:T(8,128)} %shard_map.91), kind=kLoop, calls=%fused_computation | loop fusion | flops 245760 | bytes 1474560 | tf_op jit(solution)/shard_map/reshape | solution.py:544

commit v4 on v3

--- a/solution.py
+++ b/solution.py
@@ -22,122 +22,123 @@
     ((
         ("zo", "part"), ("xo", "part"), ("xo", 1), ("zo", 1), ("X", "part", 0, 3, 0), ("X", "part", 0, 1, 0),
         ("X", "part", 0, 3, 1), ("X", "part", 0, 1, 1), ("X", 1, 0, 3, 0), ("X", 1, 0, 1, 0), ("Z", "part", 3, 0),
-        ("Z", "part", 1, 1), ("X", 1, 0, 3, 1), ("X", 1, 0, 1, 1), ("X", "part", 0, 2, 0), ("X", "part", 0, 2, 1),
-        ("YO", 0), ("Z", "part", 3, 1), ("Z", "part", 1, 0), ("xo", 0), ("X", 1, 0, 2, 0), ("X", "part", 3, 1, 0),
-        ("X", "part", 3, 3, 0), ("X", "part", 1, 1, 1), ("X", "part", 1, 3, 1), ("X", "part", 3, 3, 1),
-        ("X", 1, 0, 2, 1),
+        ("Z", "part", 1, 1), ("Z", "part", 3, 1), ("Z", "part", 1, 0), ("xo", 0), ("X", 1, 0, 3, 1),
+        ("X", 1, 0, 1, 1), ("X", "part", 0, 2, 0), ("X", "part", 0, 2, 1), ("YO", 0), ("X", "part", 3, 1, 0),
+        ("X", 1, 0, 2, 0), ("X", "part", 1, 1, 1), ("X", "part", 3, 3, 0), ("X", "part", 3, 1, 1),
+        ("X", "part", 1, 3, 1), ("X", "part", 1, 1, 0), ("X", "part", 3, 3, 1), ("X", "part", 1, 3, 0),
+        ("X", 0, 0, 1, 0), ("Z", 1, 3, 0), ("Z", 1, 1, 1), ("zo", 0), ("Y", 0, 3, 0), ("Y", 0, 1, 1),
+        ("X", 0, 0, 3, 0), ("X", 0, 0, 1, 1), ("Z", 1, 3, 1), ("Z", 1, 1, 0), ("Z", "part", 2, 0),
+        ("Z", "part", 2, 1), ("X", 0, 0, 3, 1), ("X", 1, 0, 2, 1),
     ), (
         ("zo", "part"), ("xo", "part"), ("xo", 1), ("X", "part", 0, 3, 0), ("X", "part", 0, 1, 0),
         ("X", "part", 0, 3, 1), ("X", "part", 0, 1, 1), ("X", 1, 0, 3, 0), ("X", 1, 0, 1, 0), ("X", 1, 0, 3, 1),
-        ("X", 1, 0, 1, 1), ("X", "part", 0, 2, 0), ("X", "part", 0, 2, 1), ("YO", 0), ("X", 1, 0, 2, 0),
-        ("Z", "part", 3, 0), ("Z", "part", 1, 1), ("zo", 1), ("X", 1, 0, 2, 1),
+        ("X", 1, 0, 1, 1), ("X", "part", 0, 2, 0), ("X", "part", 0, 2, 1), ("YO", 0), ("Z", "part", 3, 0),
+        ("Z", "part", 1, 1), ("zo", 1), ("X", 1, 0, 2, 0), ("X", 1, 0, 2, 1),
     ), ("pr", 1, 0)),
     ((
-        ("X", "part", 1, 3, 0), ("X", "part", 3, 1, 1), ("Y", 0, 3, 0), ("Y", 0, 1, 1), ("X", "part", 1, 1, 0),
-        ("X", 0, 0, 3, 0), ("Z", 1, 3, 0), ("Z", 1, 1, 1), ("zo", 0), ("X", 0, 0, 1, 0), ("X", 0, 0, 3, 1),
-        ("X", "part", 3, 2, 0), ("Y", 0, 3, 1), ("Y", 0, 1, 0), ("X", 0, 0, 1, 1), ("X", "part", 1, 2, 0),
-        ("X", "part", 1, 2, 1), ("YO", 1), ("Z", 1, 3, 1), ("Z", 1, 1, 0), ("X", "part", 3, 2, 1), ("YO", 3),
-        ("X", 0, 0, 2, 0), ("Z", "part", 2, 0), ("Z", "part", 2, 1), ("Y", 0, 2, 0), ("Y", 0, 2, 1),
-        ("X", 1, 3, 1, 0), ("X", 1, 3, 3, 0), ("X", 1, 1, 1, 1), ("X", 1, 1, 3, 1), ("X", 0, 0, 2, 1),
-        ("Y", 1, 3, 0), ("Y", 1, 1, 1), ("X", 1, 3, 3, 1), ("X", 1, 3, 1, 1), ("X", 1, 1, 3, 0),
-        ("X", "part", 2, 3, 0), ("X", 1, 1, 1, 0), ("Y", 1, 3, 1), ("Y", 1, 1, 0), ("X", "part", 2, 3, 1),
-        ("X", "part", 2, 1, 0), ("X", "part", 2, 1, 1), ("X", 1, 3, 2, 0), ("X", 1, 1, 2, 1), ("Y", 3, 3, 0),
-        ("X", 1, 1, 2, 0), ("Y", 3, 1, 1),
+        ("Y", 0, 3, 1), ("X", "part", 3, 2, 0), ("Y", 0, 1, 0), ("X", "part", 1, 2, 1), ("X", "part", 1, 2, 0),
+        ("YO", 1), ("X", "part", 3, 2, 1), ("YO", 3), ("X", 1, 3, 3, 0), ("X", 1, 3, 1, 0), ("Y", 0, 2, 0),
+        ("Y", 0, 2, 1), ("X", 1, 1, 3, 1), ("X", 1, 1, 1, 1), ("X", 0, 0, 2, 0), ("X", 0, 0, 2, 1), ("Y", 1, 3, 0),
+        ("Y", 1, 1, 1), ("X", 1, 3, 3, 1), ("X", 1, 3, 1, 1), ("X", 1, 1, 3, 0), ("X", 1, 1, 1, 0),
+        ("X", "part", 2, 3, 0), ("X", "part", 2, 1, 0), ("Y", 1, 3, 1), ("Y", 1, 1, 0), ("X", "part", 2, 3, 1),
+        ("X", "part", 2, 1, 1), ("X", 1, 3, 2, 0), ("X", 1, 1, 2, 1), ("Z", 1, 2, 0), ("Z", 1, 2, 1), ("Y", 3, 3, 0),
+        ("Y", 3, 1, 1), ("X", 1, 1, 2, 0), ("X", 1, 3, 2, 1),
     ), (
         ("Z", "part", 3, 1), ("Z", "part", 1, 0), ("xo", 0), ("X", "part", 3, 3, 0), ("X", "part", 3, 1, 0),
-        ("Y", 0, 3, 0), ("Y", 0, 1, 1), ("X", "part", 1, 3, 1), ("X", "part", 1, 1, 1), ("X", "part", 3, 1, 1),
+        ("X", "part", 1, 3, 1), ("X", "part", 1, 1, 1), ("Y", 0, 3, 0), ("Y", 0, 1, 1), ("X", "part", 3, 1, 1),
         ("X", "part", 3, 3, 1), ("X", "part", 1, 1, 0), ("X", "part", 1, 3, 0), ("Y", 0, 3, 1), ("Y", 0, 1, 0),
-        ("X", 0, 0, 1, 0), ("X", 0, 0, 3, 0), ("X", 0, 0, 1, 1), ("X", 0, 0, 3, 1), ("X", "part", 1, 2, 1),
-        ("X", "part", 3, 2, 0), ("Y", 0, 2, 0), ("Y", 0, 2, 1), ("X", "part", 3, 2, 1), ("YO", 3),
-        ("X", "part", 1, 2, 0), ("YO", 1), ("Z", "part", 2, 0), ("Z", "part", 2, 1), ("X", 0, 0, 2, 0),
-        ("X", 0, 0, 2, 1), ("X", "part", 2, 3, 0), ("Z", 1, 3, 0), ("X", "part", 2, 1, 0), ("Z", 1, 1, 1), ("zo", 0),
-        ("X", "part", 2, 3, 1), ("X", "part", 2, 1, 1),
+        ("X", 0, 0, 1, 0), ("X", 0, 0, 3, 0), ("Z", "part", 2, 0), ("Z", "part", 2, 1), ("X", 0, 0, 1, 1),
+        ("X", 0, 0, 3, 1), ("X", "part", 1, 2, 1), ("X", "part", 3, 2, 0), ("Y", 0, 2, 0), ("Y", 0, 2, 1),
+        ("X", "part", 3, 2, 1), ("YO", 3), ("X", "part", 1, 2, 0), ("YO", 1), ("X", "part", 2, 1, 0),
+        ("X", 0, 0, 2, 0), ("X", "part", 2, 1, 1), ("X", "part", 2, 3, 0), ("Z", 1, 3, 0), ("Z", 1, 1, 1), ("zo", 0),
+        ("X", 0, 0, 2, 1), ("X", "part", 2, 3, 1),
     ), ("un", 0)),
     ((
-        ("Z", 1, 2, 0), ("Z", 1, 2, 1), ("X", "part", 2, 2, 0), ("X", 1, 3, 2, 1),
-    ), (
-        ("Y", 3, 3, 0), ("Y", 3, 1, 1),
+        ("Z", 0, 3, 0), ("Z", 0, 1, 1), ("X", "part", 2, 2, 0), ("X", "part", 2, 2, 1), ("YO", 2), ("Z", 0, 3, 1),
+        ("Z", 0, 1, 0), ("X", 1, 2, 3, 0), ("X", 1, 2, 1, 0),
+    ), (
+        ("X", "part", 2, 2, 1), ("X", "part", 2, 2, 0), ("YO", 2), ("Y", 3, 3, 0), ("Y", 3, 1, 1),
     ), ("pr", 0, 0)),
     ((
-        ("X", "part", 2, 2, 1), ("YO", 2), ("Y", 3, 3, 1), ("Y", 3, 1, 0),
-    ), (
-        ("X", "part", 2, 2, 0), ("Z", 1, 3, 1), ("Z", 1, 1, 0), ("X", 1, 3, 1, 0), ("X", 1, 3, 3, 0), ("Y", 3, 3, 1),
-        ("Y", 3, 1, 0), ("X", 1, 1, 1, 1), ("X", 1, 1, 3, 1), ("X", "part", 2, 2, 1), ("YO", 2), ("X", 1, 3, 3, 1),
-        ("X", 1, 3, 1, 1), ("Y", 1, 3, 0), ("Y", 1, 1, 1), ("X", 1, 1, 3, 0), ("X", 1, 1, 1, 0), ("X", 1, 3, 2, 0),
-        ("X", 1, 1, 2, 1), ("Y", 1, 3, 1), ("Y", 1, 1, 0), ("X", 1, 3, 2, 1),
+        ("Y", 3, 3, 1), ("Y", 3, 1, 0),
+    ), (
+        ("X", 1, 3, 1, 0), ("X", 1, 3, 3, 0), ("Z", 1, 3, 1), ("Z", 1, 1, 0), ("X", 1, 1, 1, 1), ("X", 1, 1, 3, 1),
+        ("Y", 3, 3, 1), ("Y", 3, 1, 0), ("X", 1, 3, 2, 0), ("X", 1, 3, 1, 1), ("Y", 1, 3, 0), ("Y", 1, 1, 1),
+        ("X", 1, 3, 3, 1), ("X", 1, 1, 1, 0), ("X", 1, 1, 3, 0), ("X", 1, 1, 2, 1), ("Y", 1, 3, 1), ("Y", 1, 1, 0),
+        ("X", 1, 3, 2, 1),
     ), ("pr", 1, 3)),
     ((
-        ("Z", 0, 3, 0), ("Z", 0, 1, 1),
-    ), (
-        ("X", 1, 1, 2, 0),
+        ("X", 1, 2, 3, 1), ("X", 1, 2, 1, 1),
+    ), (
+        ("Z", 1, 2, 0), ("Z", 1, 2, 1), ("X", 1, 1, 2, 0),
     ), ("pr", 1, 1)),
     ((
-        ("X", 1, 2, 3, 0), ("X", 1, 2, 1, 0),
+        ("X", 0, 3, 3, 0), ("X", 0, 3, 1, 0),
     ), (
     ), ("ask", 1)),
     ((
-        ("Y", 1, 2, 0), ("Y", 1, 2, 1), ("Z", 0, 3, 1), ("X", 1, 2, 3, 1), ("Z", 0, 1, 0), ("X", 1, 2, 1, 1),
-    ), (
-        ("Y", 3, 2, 0), ("Y", 3, 2, 1),
+        ("Y", 1, 2, 0), ("Y", 1, 2, 1),
+    ), (
+        ("Y", 2, 3, 0), ("Y", 2, 1, 1),
     ), ("at", 1, 0)),
     ((
-        ("X", 0, 3, 3, 0), ("X", 0, 3, 1, 0),
-    ), (
-        ("Z", 1, 2, 0), ("Z", 1, 2, 1),
+        ("X", 0, 1, 3, 1), ("X", 0, 1, 1, 1), ("X", 0, 3, 3, 1), ("X", 0, 3, 1, 1),
+    ), (
+        ("X", 1, 2, 3, 0), ("X", 1, 2, 1, 0), ("Z", 0, 3, 0), ("Z", 0, 1, 1),
     ), ("at", 1, 1)),
     ((
-        ("X", 0, 1, 3, 1), ("Y", 3, 2, 0), ("X", 0, 1, 1, 1), ("Y", 3, 2, 1), ("X", 1, 2, 2, 0), ("X", 0, 3, 1, 1),
-        ("X", 0, 3, 3, 1), ("X", 0, 1, 1, 0), ("Y", 2, 3, 0), ("Y", 2, 1, 1), ("X", 0, 1, 3, 0), ("X", 1, 2, 2, 1),
-    ), (
-        ("Y", 2, 3, 0), ("Y", 2, 1, 1), ("Z", 0, 3, 0), ("Z", 0, 1, 1), ("X", 1, 2, 3, 0), ("X", 1, 2, 1, 0),
-        ("Y", 2, 3, 1), ("Y", 2, 1, 0), ("Z", 0, 3, 1), ("Z", 0, 1, 0), ("X", 1, 2, 3, 1), ("X", 1, 2, 1, 1),
-        ("X", 0, 3, 3, 0), ("X", 0, 3, 1, 0), ("Y", 1, 2, 0), ("Y", 1, 2, 1), ("X", 0, 1, 3, 1), ("X", 0, 1, 1, 1),
-        ("X", 1, 2, 2, 0), ("X", 0, 3, 1, 1), ("Y", 2, 2, 0), ("Z", 0, 2, 0), ("Y", 2, 2, 1), ("Z", 0, 2, 1),
-        ("X", 0, 3, 3, 1), ("X", 0, 1, 1, 0), ("X", 0, 1, 3, 0), ("X", 1, 2, 2, 1),
+        ("Y", 3, 2, 0), ("Y", 3, 2, 1), ("X", 0, 1, 3, 0), ("X", 0, 1, 1, 0), ("X", 1, 2, 2, 0), ("X", 1, 2, 2, 1),
+    ), (
+        ("X", 1, 2, 3, 1), ("X", 1, 2, 1, 1), ("Y", 2, 3, 1), ("Y", 2, 1, 0), ("X", 1, 2, 2, 0), ("X", 0, 3, 1, 0),
+        ("Y", 3, 2, 0), ("Y", 3, 2, 1), ("Z", 0, 3, 1), ("Z", 0, 1, 0), ("X", 0, 3, 3, 0), ("X", 0, 1, 1, 1),
+        ("X", 0, 1, 3, 1), ("X", 1, 2, 2, 1),
     ), ("pr", 1, 2)),
     ((
     ), (
+        ("Y", 1, 2, 0), ("Y", 1, 2, 1),
     ), ("at", 1, 2)),
     ((
-        ("X", 0, 3, 2, 0), ("X", 0, 1, 2, 1), ("Y", 2, 3, 1), ("Y", 2, 1, 0), ("X", 0, 3, 2, 1),
-    ), (
-        ("X", 0, 3, 2, 0), ("X", 0, 1, 2, 1),
+        ("Y", 2, 3, 0), ("Y", 2, 1, 1), ("X", 0, 3, 2, 0), ("X", 0, 1, 2, 1), ("X", 0, 1, 2, 0), ("X", 0, 3, 2, 1),
+    ), (
+        ("X", 0, 3, 3, 1), ("X", 0, 3, 1, 1), ("X", 0, 1, 3, 0), ("X", 0, 1, 1, 0),
     ), ("fin", 1)),
     ((
-        ("X", 0, 1, 2, 0), ("Z", 0, 2, 0), ("Z", 0, 2, 1), ("Y", 2, 2, 0), ("Y", 2, 2, 1),
-    ), (
-        ("X", 0, 2, 3, 0), ("X", 0, 3, 2, 1), ("X", 0, 2, 3, 1), ("X", 0, 2, 1, 0),
+        ("Y", 2, 3, 1), ("Y", 2, 1, 0), ("Z", 0, 2, 0), ("Z", 0, 2, 1), ("Y", 2, 2, 0), ("Y", 2, 2, 1),
+        ("X", 0, 2, 3, 0), ("X", 0, 2, 1, 0),
+    ), (
+        ("Y", 2, 2, 0), ("Y", 2, 2, 1), ("Z", 0, 2, 0), ("Z", 0, 2, 1), ("X", 0, 3, 2, 0), ("X", 0, 1, 2, 1),
     ), ("un", 3)),
     ((
     ), (
-        ("X", 0, 1, 2, 0), ("X", 0, 2, 1, 1),
+        ("X", 0, 3, 2, 1), ("X", 0, 1, 2, 0),
     ), ("pr", 0, 3)),
     ((
+        ("X", 0, 2, 3, 1), ("X", 0, 2, 1, 1),
     ), (
     ), ("pr", 0, 1)),
     ((
+    ), (
         ("X", 0, 2, 3, 0), ("X", 0, 2, 1, 0),
-    ), (
     ), ("ask", 0)),
     ((
+        ("X", 0, 2, 2, 0),
+    ), (
+    ), ("at", 0, 0)),
+    ((
+    ), (
         ("X", 0, 2, 3, 1), ("X", 0, 2, 1, 1),
+    ), ("un", 1)),
+    ((
+        ("X", 0, 2, 2, 1),
     ), (
         ("X", 0, 2, 2, 0),
-    ), ("at", 0, 0)),
+    ), ("at", 0, 1)),
+    ((
+    ), (
+    ), ("un", 2)),
     ((
     ), (
         ("X", 0, 2, 2, 1),
-    ), ("un", 1)),
-    ((
-        ("X", 0, 2, 2, 0),
-    ), (
-    ), ("at", 0, 1)),
-    ((
-        ("X", 0, 2, 2, 1),
-    ), (
-    ), ("un", 2)),
-    ((
-    ), (
     ), ("cv", 0)),
     ((
     ), (

time: 91.8 us -> 95.2 us (1.037)
  the two profiles are of different devices: /device:TPU:24 before, /device:TPU:33 now
where the time goes in v4:
time: 95.2 us; the launch traced here: 95.1 us
  Pallas kernels  93 us (98%)
  other arithmetic  2.04 us (2%)
    pallas_call x1, Pallas kernels, body(): pl.pallas_call(kernel, out_shape=jax.ShapeDtypeStruct((4, W, C), f32), in...  93 us
    reshape x1, other arithmetic, body(): return out.astype(bf16).reshape(4, 1, W, C)  2.04 us

profile of v4, /device:TPU:33, one launch (start us, length us, event | category | flops | bytes accessed | tf_op | source)
XLA Modules:
  0.0 95.1 jit_solution(17939107470400244851)
XLA Ops:
  0.0 93.0 %shard_map.91 = f32[4,160,384]{2,1,0:T(8,128)} custom-call(bf16[320,384]{1,0:T(8,128)(2,1)} %bitcast.7, bf16[648,384]{1,0:T(8,128)(2,1)} %bitcast.6, f32[384]{0:T(512)} %attn_gain_hbm.1, f32[384]{0:T(512)} %unit_gain_hbm.1, bf16[384,384]{1,0:T(8,128)(2,1)} %w_query_hbm.1, bf16[384,384]{1,0:T(8,128)(2,1)} %w_key_hbm.1, bf16[384,384]{1,0:T(8,128)(2,1)} %w_value_hbm.1, ...), custom_call_target="tpu_custom_call" | custom-call | tf_op jit(solution)/shard_map/pallas_call | solution.py:506
  93.1 2.0 %convert_bitcast_fusion = bf16[4,1,160,384]{3,2,1,0:T(8,128)(2,1)} fusion(f32[4,160,384]{2,1,0:T(8,128)} %shard_map.91), kind=kLoop, calls=%fused_computation | loop fusion | flops 245760 | bytes 1474560 | tf_op jit(solution)/shard_map/reshape | solution.py:545
